TPU v7x, 32 devices: a whole 2x2x4 slice. The times are simulated.
32 devices in a mesh: dp: 8 (over z, y), fsdp: 4 (over x, core).
Axes of the slice: x: 2, y: 2, z: 4, core: 2. Of those that a mesh axis runs over, the one named last changes fastest.
Arguments:
- tokens: bfloat16 [16384, 768], P(('dp', 'fsdp')), may hold values from -6 to 6
- cotangent: bfloat16 [16384, 768], P(('dp', 'fsdp')), may hold values from -6 to 6
- segment_ids: int32 [16384], P('dp'), may hold values from 0 to 24, as said below
- segment_starts: int32 [16384], P('dp'), may hold values from 0 to 2047, as said below
- padding_mask: int32 [16384], P('dp'), may hold values from 0 to 1, as said below
- lead_index: int32 [8], P('dp'), may hold values from 0 to 19
- input_weights: float32 [2, 768, 2304], P(None, ('dp', 'fsdp')), may hold values from -0.21875 to 0.21875
- input_moment: float32 [2, 768, 2304], P(None, ('dp', 'fsdp')), may hold values from -224 to 224
- input_square: float32 [2, 768, 2304], P(None, ('dp', 'fsdp')), may hold values from 737.28 to 11796.48
- output_weights: float32 [2, 768, 768], P(None, ('dp', 'fsdp')), may hold values from -0.875 to 0.875
- output_moment: float32 [2, 768, 768], P(None, ('dp', 'fsdp')), may hold values from -160 to 160
- output_square: float32 [2, 768, 768], P(None, ('dp', 'fsdp')), may hold values from 327.68 to 5242.88
- expand_weights: float32 [2, 768, 3072], P(None, ('dp', 'fsdp')), may hold values from -0.21875 to 0.21875
- expand_moment: float32 [2, 768, 3072], P(None, ('dp', 'fsdp')), may hold values from -192 to 192
- expand_square: float32 [2, 768, 3072], P(None, ('dp', 'fsdp')), may hold values from 491.52 to 8192
- shrink_weights: float32 [2, 3072, 768], P(None, ('dp', 'fsdp')), may hold values from -0.109375 to 0.109375
- shrink_moment: float32 [2, 3072, 768], P(None, ('dp', 'fsdp')), may hold values from -448 to 448
- shrink_square: float32 [2, 3072, 768], P(None, ('dp', 'fsdp')), may hold values from 2949.12 to 47185.92
- bias_vector: float32 [2, 9, 768], P(None, None, ('dp', 'fsdp')), may hold values from -4 to 4
- bias_moment: float32 [2, 9, 768], P(None, None, ('dp', 'fsdp')), may hold values from -384 to 384
- bias_square: float32 [2, 9, 768], P(None, None, ('dp', 'fsdp')), may hold values from 2048 to 32768
- lead_table: float32 [2, 20, 3072], P(None, None, ('dp', 'fsdp')), may hold values from -4 to 4
- lead_moment: float32 [2, 20, 3072], P(None, None, ('dp', 'fsdp')), may hold values from -80 to 80
- lead_square: float32 [2, 20, 3072], P(None, None, ('dp', 'fsdp')), may hold values from 102.375 to 1638
Outputs:
- out_tokens: float32 [16384, 768], P(('dp', 'fsdp'))
- in_grad: float32 [16384, 768], P(('dp', 'fsdp'))
- input_updated: float32 [2, 768, 2304], P(None, ('dp', 'fsdp'))
- input_moments: float32 [2, 768, 2304], P(None, ('dp', 'fsdp'))
- input_squares: float32 [2, 768, 2304], P(None, ('dp', 'fsdp'))
- input_copies: bfloat16 [2, 768, 2304], P(None, ('dp', 'fsdp'))
- output_updated: float32 [2, 768, 768], P(None, ('dp', 'fsdp'))
- output_moments: float32 [2, 768, 768], P(None, ('dp', 'fsdp'))
- output_squares: float32 [2, 768, 768], P(None, ('dp', 'fsdp'))
- output_copies: bfloat16 [2, 768, 768], P(None, ('dp', 'fsdp'))
- expand_updated: float32 [2, 768, 3072], P(None, ('dp', 'fsdp'))
- expand_moments: float32 [2, 768, 3072], P(None, ('dp', 'fsdp'))
- expand_squares: float32 [2, 768, 3072], P(None, ('dp', 'fsdp'))
- expand_copies: bfloat16 [2, 768, 3072], P(None, ('dp', 'fsdp'))
- shrink_updated: float32 [2, 3072, 768], P(None, ('dp', 'fsdp'))
- shrink_moments: float32 [2, 3072, 768], P(None, ('dp', 'fsdp'))
- shrink_squares: float32 [2, 3072, 768], P(None, ('dp', 'fsdp'))
- shrink_copies: bfloat16 [2, 3072, 768], P(None, ('dp', 'fsdp'))
- bias_updated: float32 [2, 9, 768], P(None, None, ('dp', 'fsdp'))
- bias_moments: float32 [2, 9, 768], P(None, None, ('dp', 'fsdp'))
- bias_squares: float32 [2, 9, 768], P(None, None, ('dp', 'fsdp'))
- bias_copies: bfloat16 [2, 9, 768], P(None, None, ('dp', 'fsdp'))
- lead_updated: float32 [2, 20, 3072], P(None, None, ('dp', 'fsdp'))
- lead_moments: float32 [2, 20, 3072], P(None, None, ('dp', 'fsdp'))
- lead_squares: float32 [2, 20, 3072], P(None, None, ('dp', 'fsdp'))
- lead_copies: bfloat16 [2, 20, 3072], P(None, None, ('dp', 'fsdp'))
Inputs may be any that keep to these rules, and one draw needn't show every extreme that they name: `segment_ids`: in each sequence of 2048 patches the window number starts at 0 and rises by one at each new window; every window but a sequence's last holds 64 to 512 consecutive patches, and some window of every sequence holds exactly 512; the last one may be cut by the sequence's end. `segment_starts`: equal for all patches of one window: the position of its first patch within the sequence. `padding_mask`: 0 exactly on the patches of a sequence's last window where it is cut by the sequence's end.
All inputs are finite; a program needn't handle non-finite values.
Results may differ from a plain program's by a relative error of at most 0.015.
Values may be sent and summed in bfloat16 or wider, within the bound.
A program may use at most 384 MiB of HBM per device.

v0:
```python
import functools
import math

import jax
import jax.numpy as jnp
from jax import lax
from jax.experimental import pallas as pl
from jax.experimental.pallas import tpu as pltpu
from jax.sharding import PartitionSpec as P

D = 768
FF = 3072
HEADS = 12
HEAD_DIM = 64
LEADS = 20
LAYERS = 2
WIN_MAX = 512
STEP = 10

EPSILON = 1e-06
NEGATIVE = -1e30
BETA_ONE = 0.5
BETA_TWO = 0.5
RATE_MATRIX = 0.08
RATE_VECTOR = 0.3
DECAY = 0.1
ADAM_EPSILON = 1e-08

MESH = pl.DeviceIdType.MESH
NZ, NY, NX = 4, 2, 2
CHIPS = NZ * NY * NX
SMALL = 256
GATHERED = (
    (4, "small", 0, 48, 0, 48, 0, 128, "zxy"),
    (0, "square", 0, 48, 0, 48, 0, 1152, "xzy"),
    (1, "square", 2304, 48, 0, 48, 0, 384, "yzx"),
    (2, "square", 3072, 48, 0, 48, 0, 768, "yzx"),
    (2, "square", 3072, 48, 0, 48, 768, 768, "zxy"),
    (3, "shrink", 0, 192, 0, 48, 0, 384, "zxy"),
    (3, "shrink", 0, 192, 48, 144, 0, 384, "zyx"),
)
SCATTERED = (
    (5, "later_in", 0, 48, 0, 48, 0, 384, "xzy"),
    (5, "later_in", 0, 48, 0, 48, 384, 384, "yzx"),
    (5, "later_in", 0, 48, 0, 48, 768, 384, "zxy"),
    (6, "later_out", 0, 48, 0, 48, 0, 384, "zyx"),
    (7, "later_expand", 0, 48, 0, 48, 0, 384, "xzy"),
    (7, "later_expand", 0, 48, 0, 48, 384, 384, "yzx"),
    (7, "later_expand", 0, 48, 0, 48, 768, 384, "zxy"),
    (7, "later_expand", 0, 48, 0, 48, 1152, 384, "zyx"),
    (2, "expand", 0, 48, 0, 48, 0, 768, "xzy"),
    (2, "expand", 0, 48, 0, 48, 768, 768, "yzx"),
    (3, "shrink", 0, 192, 0, 96, 0, 384, "zxy"),
    (3, "shrink", 0, 192, 96, 96, 0, 384, "zyx"),
    (0, "in", 0, 48, 0, 48, 0, 384, "xzy"),
    (0, "in", 0, 48, 0, 48, 384, 384, "yzx"),
    (0, "in", 0, 48, 0, 48, 768, 384, "zxy"),
    (1, "out", 0, 48, 0, 48, 0, 384, "zyx"),
    (4, "small", 0, 48, 0, 48, 0, 128, "zyx"),
)
LAG = (0.0,) * 4 + (0.5,) * 4 + (1.0,) * 2 + (1.5,) * 2 + (2.0,) * 5
WIDTHS = (2304, 768, 3072, 768, SMALL, 2304, 768, 3072)
OWN_ROWS = (24, 24, 24, 96, 24, 24, 24, 24)
WHOLES = {"square": (768, 6144), "shrink": (3072, 768), "small": (768, SMALL)}
AXIS = {"z": 0, "y": 1, "x": 2}


def place():
    dp, fs = lax.axis_index("dp"), lax.axis_index("fsdp")
    return lax.div(dp, NY), lax.rem(dp, NY), lax.div(fs, 2), lax.rem(fs, 2)


def device(z, y, x, core):
    return (z * NY + y, x * 2 + core)


def offsets():
    found = [
        (dz, dy, dx)
        for dz in range(1 - NZ, NZ)
        for dy in range(NY)
        for dx in range(NX)
    ]
    return sorted(found, key=lambda d: (abs(d[0]) + d[1] + d[2], abs(d[0])))


def last_axis(order, away):
    last = -1
    for number, axis in enumerate(order):
        if away[AXIS[axis]] != 0:
            last = number
    return last


def children(order, away):
    last = last_axis(order, away)
    found = []
    for number, axis in enumerate(order):
        if number < last:
            continue
        if axis == "z":
            if number > last:
                found += ["up", "down"]
            else:
                found += ["up"] if away[0] < 0 else ["down"]
        elif number > last:
            found.append(axis)
    return found


def exists(side, z):
    return {"up": z < NZ - 1, "down": z > 0}.get(side)


def neighbour(side, spot):
    z, y, x, core = spot
    return {
        "up": device(z + 1, y, x, core),
        "down": device(z - 1, y, x, core),
        "y": device(z, 1 - y, x, core),
        "x": device(z, y, 1 - x, core),
        "core": device(z, y, x, 1 - core),
    }[side]


def guarded(condition, action):
    if condition is None:
        action()
    else:
        pl.when(condition)(action)


def both(first, second):
    if first is None:
        return second
    if second is None:
        return first
    return first & second


def greet(spot):
    barrier = pltpu.get_barrier_semaphore()
    z, y, x, core = spot
    sides = [(neighbour(side, spot), exists(side, z)) for side in ("up", "down", "x", "y", "core")]
    count = 3
    for target, there in sides:

        def hello(target=target):
            pl.semaphore_signal(barrier, inc=1, device_id=target, device_id_type=MESH)

        guarded(there, hello)
        if there is not None:
            count = count + jnp.where(there, 1, 0)
    pl.semaphore_wait(barrier, count)


def source_of(spot, away):
    z, y, x, _ = spot
    sz = z + away[0]
    sy = 1 - y if away[1] else y
    sx = 1 - x if away[2] else x
    valid = None
    if away[0] > 0:
        valid = sz < NZ
    elif away[0] < 0:
        valid = sz >= 0
    return sz, sy, sx, valid


def chip_number(sz, sy, sx):
    return (sz * NY + sy) * NX + sx


def aligned(value, by):
    return value if isinstance(value, int) else pl.multiple_of(value, by)


def piece_view(ref, piece, chip, core):
    number, _, base, chip_rows, low, rows, column, columns, _ = piece
    half = WIDTHS[number] // 2
    return ref.at[
        pl.ds(aligned(chip * chip_rows + low, 16), rows),
        pl.ds(aligned(base + core * half + column, 128), columns),
    ]


class Job:
    def __init__(self, pieces):
        self.pieces = pieces
        self.numbers = tuple(dict.fromkeys(p[0] for p in pieces))
        self.arrays = tuple(dict.fromkeys(p[1] for p in pieces))

    def scratch_of(self, rows, dtype):
        return [pltpu.VMEM((rows * OWN_ROWS[n], WIDTHS[n] // 2), dtype) for n in self.numbers]


class GatherJob(Job):
    def __init__(self, pieces, layer):
        super().__init__(pieces)
        self.layer = layer
        self.inputs = len(self.numbers)
        self.outputs = tuple(jax.ShapeDtypeStruct(WHOLES[a], jnp.bfloat16) for a in self.arrays)
        count = len(pieces)
        self.scratch = (
            self.scratch_of(1, jnp.float32)
            + self.scratch_of(1, jnp.float32)
            + self.scratch_of(2, jnp.bfloat16)
            + [
                pltpu.SemaphoreType.DMA((8,)),
                pltpu.SemaphoreType.DMA((8,)),
                pltpu.SemaphoreType.DMA((8,)),
                pltpu.SemaphoreType.DMA((count,)),
                pltpu.SemaphoreType.DMA((count, 4)),
                pltpu.SemaphoreType.DMA((count, CHIPS)),
                pltpu.SemaphoreType.DMA((count,)),
                pltpu.SemaphoreType.DMA((count,)),
            ]
        )

    def bind(self, inputs, outputs, scratch):
        pieces, numbers, layer = self.pieces, self.numbers, self.layer
        many = len(numbers)
        take = iter(scratch)
        named = lambda: dict(zip(numbers, [next(take) for _ in range(many)]))
        masters = dict(zip(numbers, inputs))
        wholes = dict(zip(self.arrays, outputs))
        mine, theirs, blocks = named(), named(), named()
        local_sem, pair_send, pair_recv, store_sem, send_sem, recv_sem, core_send, core_recv = take
        spot = place()
        z, y, x, core = spot
        me = chip_number(z, y, x)
        partner = neighbour("core", spot)

        def columns_of(number, side):
            half = WIDTHS[number] // 2
            which = 0 if number == 4 else layer
            return masters[number].at[which, :, pl.ds(aligned(side * half, 128), half)]

        def load(number):
            return pltpu.make_async_copy(columns_of(number, core), mine[number], local_sem.at[number])

        def swap(number):
            return pltpu.make_async_remote_copy(
                src_ref=columns_of(number, 1 - core),
                dst_ref=theirs[number],
                send_sem=pair_send.at[number],
                recv_sem=pair_recv.at[number],
                device_id=partner,
                device_id_type=MESH,
            )

        def relay(index, away, source, view):
            piece = pieces[index]
            for side in children(piece[8], away):

                def send(side=side):
                    pltpu.make_async_remote_copy(
                        src_ref=view,
                        dst_ref=piece_view(wholes[piece[1]], piece, source, core),
                        send_sem=send_sem.at[index, ("up", "down", "x", "y").index(side)],
                        recv_sem=recv_sem.at[index, source],
                        device_id=neighbour(side, spot),
                        device_id_type=MESH,
                    ).start()

                guarded(exists(side, z), send)
            pltpu.make_async_remote_copy(
                src_ref=view,
                dst_ref=piece_view(wholes[piece[1]], piece, source, core),
                send_sem=core_send.at[index],
                recv_sem=core_recv.at[index],
                device_id=partner,
                device_id_type=MESH,
            ).start()

        def own_view(index):
            piece = pieces[index]
            return blocks[piece[0]].at[pl.ds(piece[4], piece[5]), pl.ds(piece[6], piece[7])]

        def store(index):
            piece = pieces[index]
            return pltpu.make_async_copy(
                own_view(index), piece_view(wholes[piece[1]], piece, me, core), store_sem.at[index]
            )

        def start():
            for number in numbers:
                load(number).start()
            for number in numbers:
                swap(number).start()

        def own(number):
            load(number).wait()
            swap(number).wait_recv()
            own_rows, other_rows = mine[number][...], theirs[number][...]
            is_first = core == 0
            block = jnp.concatenate(
                [jnp.where(is_first, own_rows, other_rows), jnp.where(is_first, other_rows, own_rows)],
                axis=0,
            )
            blocks[number][...] = block.astype(jnp.bfloat16)
            for index, piece in enumerate(pieces):
                if piece[0] == number:
                    store(index).start()
                    relay(index, (0, 0, 0), me, own_view(index))

        def event(away, index):
            piece = pieces[index]
            sz, sy, sx, valid = source_of(spot, away)
            source = chip_number(sz, sy, sx)

            def arrival():
                view = piece_view(wholes[piece[1]], piece, source, core)
                pltpu.make_async_remote_copy(
                    src_ref=view,
                    dst_ref=view,
                    send_sem=send_sem.at[index, 0],
                    recv_sem=recv_sem.at[index, source],
                    device_id=partner,
                    device_id_type=MESH,
                ).wait_recv()
                relay(index, away, source, view)

            guarded(valid, arrival)

        def finish():
            for index in range(len(pieces)):
                store(index).wait()
            for number in numbers:
                swap(number).wait_send()
            for index, piece in enumerate(pieces):
                number, rows, columns = piece[0], piece[5], piece[7]

                def span(chunks, core_at, piece=piece, number=number, rows=rows, columns=columns):
                    half = WIDTHS[number] // 2
                    first = aligned(piece[2] + core_at * half + piece[6], 128)
                    return wholes[piece[1]].at[pl.ds(0, chunks * rows), pl.ds(first, columns)]

                def wait_send(chunks, sem, index=index, span=span):
                    pltpu.make_async_remote_copy(
                        src_ref=span(chunks, core),
                        dst_ref=span(chunks, core),
                        send_sem=sem,
                        recv_sem=recv_sem.at[index, 0],
                        device_id=partner,
                        device_id_type=MESH,
                    ).wait_send()

                before = 1
                for axis in piece[8]:
                    if axis == "z":
                        for at in range(NZ):

                            @pl.when(z == at)
                            def _(at=at, before=before, index=index, wait_send=wait_send):
                                if at < NZ - 1:
                                    wait_send(before * (at + 1), send_sem.at[index, 0])
                                if at > 0:
                                    wait_send(before * (NZ - at), send_sem.at[index, 1])

                        before *= NZ
                    else:
                        wait_send(before, send_sem.at[index, 2 if axis == "x" else 3])
                        before *= 2
                wait_send(CHIPS, core_send.at[index])
                pltpu.make_async_remote_copy(
                    src_ref=span(CHIPS, 1 - core),
                    dst_ref=span(CHIPS, 1 - core),
                    send_sem=core_send.at[index],
                    recv_sem=core_recv.at[index],
                    device_id=partner,
                    device_id_type=MESH,
                ).wait_recv()

        actions = [start] + [functools.partial(own, number) for number in numbers]
        for away in offsets():
            if away != (0, 0, 0):
                actions += [functools.partial(event, away, index) for index in range(len(pieces))]
        return actions + [finish]


def slot_of(order, side, source):
    sizes = {"z": NZ, "y": NY, "x": NX}
    base = 0
    ahead = 1
    number = 0
    for axis in order:
        at = source[AXIS[axis]]
        for here in ["up", "down"] if axis == "z" else [axis]:
            if axis == "z":
                if here == side:
                    return base + number * NZ + at
                base += ahead * NZ
            else:
                if here == side:
                    return base + number
                base += ahead
        number = number * sizes[axis] + at
        ahead *= sizes[axis]
    return base


def slot_count(order):
    return slot_of(order, None, (0, 0, 0))


class ScatterJob(Job):
    def __init__(self, pieces):
        super().__init__(pieces)
        self.inputs = len(self.arrays)
        self.first = {}
        width = 0
        for number in self.numbers:
            if number != 3:
                self.first[number] = width
                width += WIDTHS[number]
        self.first[3] = 0
        self.outputs = (
            jax.ShapeDtypeStruct((OWN_ROWS[0], width), jnp.float32),
            jax.ShapeDtypeStruct((OWN_ROWS[3], WIDTHS[3]), jnp.float32),
        )
        count = len(pieces)
        most = max(slot_count(p[8]) for p in pieces)
        self.scratch = (
            self.scratch_of(32, jnp.bfloat16)
            + self.scratch_of(32, jnp.bfloat16)
            + self.scratch_of(2, jnp.float32)
            + self.scratch_of(1, jnp.float32)
            + [pltpu.VMEM((slot_count(p[8]), p[5], p[7]), jnp.bfloat16) for p in pieces]
            + [
                pltpu.SemaphoreType.DMA((8,)),
                pltpu.SemaphoreType.DMA((8,)),
                pltpu.SemaphoreType.DMA((8,)),
                pltpu.SemaphoreType.DMA((count, CHIPS)),
                pltpu.SemaphoreType.DMA((count, most)),
                pltpu.SemaphoreType.DMA((8,)),
                pltpu.SemaphoreType.DMA((8,)),
                pltpu.SemaphoreType.DMA((16,)),
            ]
        )

    def bind(self, inputs, outputs, scratch):
        pieces, numbers = self.pieces, self.numbers
        many = len(numbers)
        take = iter(scratch)
        named = lambda: dict(zip(numbers, [next(take) for _ in range(many)]))
        partials = dict(zip(self.arrays, inputs))
        outs = {n: outputs[1 if n == 3 else 0] for n in numbers}
        starts = self.first
        own, pair, total, handed = named(), named(), named(), named()
        slots = [next(take) for _ in pieces]
        own_sem, pair_send, pair_recv, send_sem, recv_sem, end_send, end_recv, out_sem = take
        base = {p[0]: p[2] for p in pieces}
        array = {p[0]: p[1] for p in pieces}
        spot = place()
        z, y, x, core = spot
        partner = neighbour("core", spot)

        def columns_of(number, side):
            half = WIDTHS[number] // 2
            first = aligned(base[number] + side * half, 128)
            return partials[array[number]].at[:, pl.ds(first, half)]

        def load(number):
            return pltpu.make_async_copy(columns_of(number, core), own[number], own_sem.at[number])

        def swap(number):
            return pltpu.make_async_remote_copy(
                src_ref=columns_of(number, 1 - core),
                dst_ref=pair[number],
                send_sem=pair_send.at[number],
                recv_sem=pair_recv.at[number],
                device_id=partner,
                device_id_type=MESH,
            )

        def start():
            for number in numbers:
                load(number).start()
                swap(number).start()

        def ready(number):
            load(number).wait()
            swap(number).wait_recv()

        def view_of(piece, source):
            _, _, _, chip_rows, low, rows, column, columns, _ = piece
            return pl.ds(aligned(source * chip_rows + low, 16), rows), pl.ds(column, columns)

        def event(away, index):
            piece = pieces[index]
            number, _, _, chip_rows, low, rows, column, columns, order = piece
            sz, sy, sx, valid = source_of(spot, away)
            where = (sz, sy, sx)
            source = chip_number(sz, sy, sx)
            last = last_axis(order, away)

            def act():
                kids = children(order, away)
                for side in kids:

                    def arrived(side=side):
                        slot = slot_of(order, side, where)
                        pltpu.make_async_remote_copy(
                            src_ref=slots[index].at[slot],
                            dst_ref=slots[index].at[slot],
                            send_sem=send_sem.at[index, 0],
                            recv_sem=recv_sem.at[index, slot],
                            device_id=partner,
                            device_id_type=MESH,
                        ).wait_recv()

                    guarded(exists(side, z), arrived)
                view = view_of(piece, source)
                value = own[number][view].astype(jnp.float32) + pair[number][view].astype(jnp.float32)
                for side in kids:
                    landed = slots[index][slot_of(order, side, where)].astype(jnp.float32)
                    there = exists(side, z)
                    value = value + (landed if there is None else jnp.where(there, landed, 0.0))
                if last < 0:
                    total[number][pl.ds(low, rows), pl.ds(column, columns)] = value
                    return
                pair[number][view] = value.astype(jnp.bfloat16)
                axis = order[last]
                if axis == "z":
                    side = "up" if away[0] < 0 else "down"
                    parent = neighbour("down" if away[0] < 0 else "up", spot)
                else:
                    side = axis
                    parent = neighbour(axis, spot)
                slot = slot_of(order, side, where)
                pltpu.make_async_remote_copy(
                    src_ref=pair[number].at[view],
                    dst_ref=slots[index].at[slot],
                    send_sem=send_sem.at[index, source],
                    recv_sem=recv_sem.at[index, slot],
                    device_id=parent,
                    device_id_type=MESH,
                ).start()

            guarded(valid, act)

        def end(number):
            rows = OWN_ROWS[number]
            return pltpu.make_async_remote_copy(
                src_ref=total[number].at[pl.ds(aligned((1 - core) * rows, 8), rows)],
                dst_ref=handed[number],
                send_sem=end_send.at[number],
                recv_sem=end_recv.at[number],
                device_id=partner,
                device_id_type=MESH,
            )

        def write(number, other):
            half = WIDTHS[number] // 2
            rows = OWN_ROWS[number]
            source = handed[number] if other else total[number].at[pl.ds(aligned(core * rows, 8), rows)]
            side = 1 - core if other else core
            return pltpu.make_async_copy(
                source,
                outs[number].at[:, pl.ds(aligned(starts[number] + side * half, 128), half)],
                out_sem.at[number + 8 * other],
            )

        def finish():
            for number in numbers:
                end(number).start()
            for number in numbers:
                write(number, 0).start()
            for number in numbers:
                end(number).wait_recv()
                write(number, 1).start()
            for number in numbers:
                write(number, 0).wait()
                write(number, 1).wait()
                end(number).wait_send()
                swap(number).wait_send()
            for index, piece in enumerate(pieces):
                for away in offsets():
                    if away == (0, 0, 0):
                        continue
                    sz, sy, sx, valid = source_of(spot, away)
                    source = chip_number(sz, sy, sx)

                    def sent(index=index, piece=piece, source=source):
                        pltpu.make_async_remote_copy(
                            src_ref=pair[piece[0]].at[view_of(piece, source)],
                            dst_ref=slots[index].at[0],
                            send_sem=send_sem.at[index, source],
                            recv_sem=recv_sem.at[index, 0],
                            device_id=partner,
                            device_id_type=MESH,
                        ).wait_send()

                    guarded(valid, sent)

        actions = [start]
        known = set()
        level = lambda away: NZ + 1 - (abs(away[0]) + away[1] + away[2])
        events = [
            (level(away) + LAG[index], index, place_at, away)
            for place_at, away in enumerate(reversed(offsets()))
            for index in range(len(pieces))
        ]
        for _, index, _, away in sorted(events):
            number = pieces[index][0]
            if number not in known:
                known.add(number)
                actions.append(functools.partial(ready, number))
            actions.append(functools.partial(event, away, index))
        return actions + [finish]


def alone(job, arrays, name, ident):
    anywhere = pl.BlockSpec(memory_space=pl.ANY)

    def kernel(*refs):
        first, second = job.inputs, job.inputs + len(job.outputs)
        greet(place())
        for action in job.bind(refs[:first], refs[first:second], refs[second:]):
            action()

    return pl.pallas_call(
        kernel,
        out_shape=job.outputs,
        in_specs=[anywhere] * job.inputs,
        out_specs=tuple([anywhere] * len(job.outputs)),
        scratch_shapes=job.scratch,
        name=name,
        compiler_params=pltpu.CompilerParams(
            collective_id=ident, has_side_effects=True, vmem_limit_bytes=60 << 20
        ),
        cost_estimate=pl.CostEstimate(flops=0, bytes_accessed=int(2e8), transcendentals=0),
    )(*arrays)


def normalize(values):
    centred = values - jnp.mean(values, axis=-1, keepdims=True)
    inverse = lax.rsqrt(jnp.mean(centred * centred, axis=-1, keepdims=True) + EPSILON)
    return (centred * inverse, inverse)


def normalize_back(grad_normed, normed, inverse):
    return inverse * (
        grad_normed
        - jnp.mean(grad_normed, axis=-1, keepdims=True)
        - normed * jnp.mean(grad_normed * normed, axis=-1, keepdims=True)
    )


def rotary_tables(relative):
    lane = jnp.arange(2 * HEAD_DIM, dtype=jnp.int32)
    indices = (lane % (HEAD_DIM // 2)).astype(jnp.float32)
    frequency = jnp.exp(indices * (-2.0 * math.log(10000.0) / HEAD_DIM))
    phase = relative.astype(jnp.float32)[:, None] * frequency[None, :]
    sign = jnp.where(lane % HEAD_DIM < HEAD_DIM // 2, -1.0, 1.0)
    return jnp.cos(phase), jnp.sin(phase) * sign[None, :]


BAND = 128
VARIANTS = (3, 4, 5, 6, 7, 9)
STEP_COLUMNS = 384
BLOCK = 512
F32 = jnp.float32
BF16 = jnp.bfloat16
MATMUL = (((1,), (0,)), ((), ()))
MATMUL_RIGHT = (((1,), (1,)), ((), ()))
MATMUL_LEFT = (((0,), (0,)), ((), ()))


def product(left, right, dims=MATMUL):
    return lax.dot_general(left, right, dims, preferred_element_type=F32)


def vmem(limit=56):
    return pltpu.CompilerParams(vmem_limit_bytes=limit << 20)


def cost(flops, moved):
    return pl.CostEstimate(flops=int(flops), bytes_accessed=int(moved), transcendentals=0)


def swap_halves(values):
    lane = lax.broadcasted_iota(jnp.int32, values.shape, 1)
    low = lax.rem(lane, HEAD_DIM) < HEAD_DIM // 2
    return jnp.where(
        low,
        pltpu.roll(values, 2 * HEAD_DIM - HEAD_DIM // 2, 1),
        pltpu.roll(values, HEAD_DIM // 2, 1),
    )


def turn(values, cosine, sine):
    parts = []
    for at in range(0, values.shape[1], 128):
        part = values[:, at : at + 128]
        parts.append(part * cosine + swap_halves(part) * sine)
    return jnp.concatenate(parts, axis=1)


def beside():
    dp, fs = lax.axis_index("dp"), lax.axis_index("fsdp")
    return ((dp, fs - 1), fs > 0), ((dp, fs + 1), fs < lax.axis_size("fsdp") - 1)


def greet_beside():
    barrier = pltpu.get_barrier_semaphore()
    count = 0
    for device_at, there in beside():

        @pl.when(there)
        def _(device_at=device_at):
            pl.semaphore_signal(barrier, inc=1, device_id=device_at, device_id_type=MESH)

        count = count + jnp.where(there, 1, 0)
    pl.semaphore_wait(barrier, count)


def halo_copies(sources, landing, send_sem, recv_sem):
    return [
        (
            there,
            pltpu.make_async_remote_copy(
                src_ref=sources[side],
                dst_ref=landing.at[1 - side],
                send_sem=send_sem.at[side],
                recv_sem=recv_sem.at[1 - side],
                device_id=device_at,
                device_id_type=MESH,
            ),
        )
        for side, (device_at, there) in enumerate(beside())
    ]


def halo_start(sources, landing, send_sem, recv_sem):
    for there, copy in halo_copies(sources, landing, send_sem, recv_sem):
        pl.when(there)(copy.start)


def halo_wait(sources, landing, send_sem, recv_sem):
    sides = beside()
    for side, (there, copy) in enumerate(halo_copies(sources, landing, send_sem, recv_sem)):
        pl.when(there)(copy.wait_send)
        device_at, _ = sides[side]

        @pl.when(there)
        def _(side=side, device_at=device_at):
            pltpu.make_async_remote_copy(
                src_ref=sources[side],
                dst_ref=landing.at[side],
                send_sem=send_sem.at[side],
                recv_sem=recv_sem.at[side],
                device_id=device_at,
                device_id_type=MESH,
            ).wait_recv()

        @pl.when(jnp.logical_not(there))
        def _(side=side):
            landing[side] = jnp.zeros(landing.shape[1:], landing.dtype)


def project_kernel(
    x_ref, w_ref, bias_ref, mod_ref, cos_ref, sin_ref, q_ref, own_ref, low_ref, high_ref, h_ref, halo_ref,
    mine, landing, send_sem, recv_sem,
):
    step = pl.program_id(0)
    rows = x_ref.shape[0]

    @pl.when(step == 0)
    def _():
        normed, _ = normalize(x_ref[...].astype(F32))
        hidden_in = (normed * (1.0 + mod_ref[0, 1:2]) + mod_ref[0, 0:1]).astype(BF16)
        mine[...] = hidden_in
        h_ref[...] = hidden_in
        greet_beside()
        halo_start((mine, mine), landing, send_sem, recv_sem)

    def own_turned(y):
        return turn(y, cos_ref[WIN_MAX : WIN_MAX + rows], sin_ref[WIN_MAX : WIN_MAX + rows]).astype(BF16)

    @pl.when(step < 6)
    def _():
        y = product(mine[...], w_ref[...]) + bias_ref[0]

        @pl.when(step < 2)
        def _():
            q_ref[...] = own_turned(y)

        @pl.when((step >= 2) & (step < 4))
        def _():
            own_ref[0] = own_turned(y)

        @pl.when(step >= 4)
        def _():
            own_ref[0] = y.astype(BF16)

    @pl.when(step == 6)
    def _():
        halo_wait((mine, mine), landing, send_sem, recv_sem)
        halo_ref[...] = landing[...]

    @pl.when(step >= 6)
    def _():
        for side, out_ref, first in ((0, low_ref, 0), (1, high_ref, WIN_MAX + rows)):
            y = product(landing[side], w_ref[...]) + bias_ref[0]

            @pl.when(step < 8)
            def _(y=y, out_ref=out_ref, first=first):
                table = slice(first, first + WIN_MAX)
                out_ref[0] = turn(y, cos_ref[table], sin_ref[table]).astype(BF16)

            @pl.when(step >= 8)
            def _(y=y, out_ref=out_ref):
                out_ref[0] = y.astype(BF16)


def project(layer, stream, square, bias, modulation, cosine, sine, ident):
    rows = stream.shape[0]
    whole = lambda shape: pl.BlockSpec(shape, lambda c: (0,) * len(shape))

    def halves(first):
        def index(c):
            at = jnp.clip(c - first, 0, 3)
            return (at // 2, 0, at % 2)

        return pl.BlockSpec((1, rows, STEP_COLUMNS), index)

    column = lambda c: (0, jnp.where(c < 6, c, c - 4))
    pair = jax.ShapeDtypeStruct((2, rows, D), BF16)
    single = jax.ShapeDtypeStruct((rows, D), BF16)
    return pl.pallas_call(
        project_kernel,
        grid=(10,),
        in_specs=[
            whole((rows, D)),
            pl.BlockSpec((D, STEP_COLUMNS), column),
            pl.BlockSpec((1, 1, STEP_COLUMNS), lambda c: (layer, *column(c))),
            pl.BlockSpec((1, 4, D), lambda c: (layer, 0, 0)),
            whole((rows + 2 * WIN_MAX, 128)),
            whole((rows + 2 * WIN_MAX, 128)),
        ],
        out_specs=(
            pl.BlockSpec((rows, STEP_COLUMNS), lambda c: (0, jnp.minimum(c, 1))),
            halves(2),
            halves(6),
            halves(6),
            whole((rows, D)),
            whole((2, rows, D)),
        ),
        out_shape=(single, pair, pair, pair, single, pair),
        scratch_shapes=[
            pltpu.VMEM((rows, D), BF16),
            pltpu.VMEM((2, rows, D), BF16),
            pltpu.SemaphoreType.DMA((2,)),
            pltpu.SemaphoreType.DMA((2,)),
        ],
        compiler_params=pltpu.CompilerParams(
            vmem_limit_bytes=56 << 20, collective_id=ident, has_side_effects=True
        ),
        cost_estimate=cost(2 * rows * D * 7 * D, 8e6),
        name="project",
    )(stream, square, bias, modulation, cosine, sine)


def stack_heads(pair):
    lane = lax.broadcasted_iota(jnp.int32, pair.shape, 1)
    zero = jnp.zeros_like(pair)
    return jnp.concatenate(
        [jnp.where(lane < HEAD_DIM, pair, zero), jnp.where(lane < HEAD_DIM, zero, pair)], axis=0
    )


def merge_heads(stacked):
    rows = stacked.shape[0] // 2
    lane = lax.broadcasted_iota(jnp.int32, (rows, stacked.shape[1]), 1)
    return jnp.where(lane < HEAD_DIM, stacked[:rows], stacked[rows:])


def over_bands(bounds_ref, count, action):
    def one(number, carry):
        low, need = bounds_ref[0, number], bounds_ref[1, number]
        before = 0
        for size in VARIANTS:

            @pl.when((need > before) & (need <= size))
            def _(size=size):
                start = jnp.minimum(low, count - size) * BAND
                action(pl.multiple_of(number * BAND, BAND), pl.multiple_of(start, BAND), size * BAND)

            before = size
        return carry

    lax.fori_loop(0, bounds_ref.shape[1], one, 0)


PAIRS = 2
LANES = 128 * PAIRS


def load_band(ext, low_ref, own_ref, high_ref):
    rows = own_ref.shape[1]
    for at in range(2):
        ext[at, :WIN_MAX] = low_ref[at]
        ext[at, WIN_MAX : WIN_MAX + rows] = own_ref[at]
        ext[at, WIN_MAX + rows :] = high_ref[at]


def attend_kernel(bounds_ref, q_ref, low_ref, own_ref, high_ref, idq_ref, idk_ref, o_ref, lse_ref, ext):
    rows = own_ref.shape[1]
    load_band(ext, low_ref, own_ref, high_ref)

    def block(first, start, size):
        mine = pl.ds(first, BAND)
        band = pl.ds(start, size)
        ids = idq_ref[mine, :]
        allowed = jnp.concatenate([ids] * (size // BAND), axis=1) == idk_ref[0:1, band]
        allowed = jnp.concatenate([allowed, allowed], axis=0)
        pairs = range(PAIRS)
        lanes = [slice(128 * p, 128 * p + 128) for p in pairs]
        queries = [stack_heads(q_ref[mine, lanes[p]]) * jnp.asarray(HEAD_DIM**-0.5, BF16) for p in pairs]
        scores = [product(queries[p], ext[0, band, lanes[p]], MATMUL_RIGHT) for p in pairs]
        scores = [jnp.where(allowed, scores[p], NEGATIVE) for p in pairs]
        peaks = [jnp.max(scores[p], axis=1, keepdims=True) for p in pairs]
        weights = [jnp.exp(scores[p] - peaks[p]) for p in pairs]
        totals = [jnp.sum(weights[p], axis=1, keepdims=True) for p in pairs]
        mixed = [product(weights[p].astype(BF16), ext[1, band, lanes[p]]) for p in pairs]
        for p in pairs:
            o_ref[mine, lanes[p]] = merge_heads(mixed[p] * (1.0 / totals[p])).astype(BF16)
            wide = jnp.broadcast_to(peaks[p] + jnp.log(totals[p]), (2 * BAND, BAND))
            lse_ref[p, 0:1, mine] = wide[:BAND].T[0:1]
            lse_ref[p, 1:2, mine] = wide[BAND:].T[0:1]

    over_bands(bounds_ref, (rows + 2 * WIN_MAX) // BAND, block)


def pair_spec(rows):
    return pl.BlockSpec((2, rows, LANES), lambda j, b: (0, 0, j))


def attend(bounds, queries, low, own, high, ids_query, ids_key):
    rows = queries.shape[0]
    wide = rows + 2 * WIN_MAX
    column = pl.BlockSpec((rows, LANES), lambda j, b: (0, j))
    return pl.pallas_call(
        attend_kernel,
        grid_spec=pltpu.PrefetchScalarGridSpec(
            num_scalar_prefetch=1,
            grid=(D // LANES,),
            in_specs=[
                column,
                pair_spec(WIN_MAX),
                pair_spec(rows),
                pair_spec(WIN_MAX),
                pl.BlockSpec((rows, 128), lambda j, b: (0, 0)),
                pl.BlockSpec((8, wide), lambda j, b: (0, 0)),
            ],
            out_specs=(column, pl.BlockSpec((PAIRS, 8, rows), lambda j, b: (j, 0, 0))),
            scratch_shapes=[pltpu.VMEM((2, wide, LANES), BF16)],
        ),
        out_shape=(
            jax.ShapeDtypeStruct((rows, D), BF16),
            jax.ShapeDtypeStruct((HEADS // 2, 8, rows), F32),
        ),
        compiler_params=vmem(),
        cost_estimate=cost(5e9, 8e6),
        name="attend",
    )(bounds, queries, low, own, high, ids_query, ids_key)


def attend_back_kernel(
    bounds_ref, q_ref, g_ref, o_ref, lse_ref, low_ref, own_ref, high_ref, idq_ref, idk_ref,
    cos_ref, sin_ref, dq_ref, dlow_ref, down_ref, dhigh_ref, ext, dext,
):
    rows = own_ref.shape[1]
    load_band(ext, low_ref, own_ref, high_ref)
    dext[...] = jnp.zeros_like(dext)

    def delta_of(mine, lanes):
        both_heads = (g_ref[mine, lanes].astype(F32) * o_ref[mine, lanes].astype(F32)).T
        return jnp.concatenate(
            [
                jnp.sum(both_heads[:HEAD_DIM], axis=0, keepdims=True),
                jnp.sum(both_heads[HEAD_DIM:], axis=0, keepdims=True),
            ],
            axis=1,
        )

    def block(first, start, size):
        mine = pl.ds(first, BAND)
        band = pl.ds(start, size)
        ids = idk_ref[band, :] == idq_ref[0:1, mine]
        allowed = jnp.concatenate([ids, ids], axis=1)
        pairs = range(PAIRS)
        lanes = [slice(128 * p, 128 * p + 128) for p in pairs]
        queries = [stack_heads(q_ref[mine, lanes[p]]) * jnp.asarray(HEAD_DIM**-0.5, BF16) for p in pairs]
        grads = [stack_heads(g_ref[mine, lanes[p]]) for p in pairs]
        keys = [ext[0, band, lanes[p]] for p in pairs]
        scores = [product(keys[p], queries[p], MATMUL_RIGHT) for p in pairs]
        grad_weights = [product(ext[1, band, lanes[p]], grads[p], MATMUL_RIGHT) for p in pairs]
        lse = [
            jnp.concatenate([lse_ref[p, 0:1, mine], lse_ref[p, 1:2, mine]], axis=1) for p in pairs
        ]
        deltas = [delta_of(mine, lanes[p]) for p in pairs]
        weights = [jnp.where(allowed, jnp.exp(scores[p] - lse[p]), 0.0) for p in pairs]
        grad_scores = [(weights[p] * (grad_weights[p] - deltas[p])).astype(BF16) for p in pairs]
        table = pl.ds(pl.multiple_of(first + WIN_MAX, BAND), BAND)
        cosine, sine = cos_ref[table, :], -sin_ref[table, :]
        for p in pairs:
            dext[0, band, lanes[p]] += product(grad_scores[p], queries[p])
            dext[1, band, lanes[p]] += product(weights[p].astype(BF16), grads[p])
            turned = merge_heads(product(grad_scores[p], keys[p], MATMUL_LEFT)) * HEAD_DIM**-0.5
            dq_ref[mine, lanes[p]] = turn(turned, cosine, sine).astype(BF16)

    over_bands(bounds_ref, (rows + 2 * WIN_MAX) // BAND, block)
    for out_ref, part in (
        (dlow_ref, slice(0, WIN_MAX)),
        (down_ref, slice(WIN_MAX, WIN_MAX + rows)),
        (dhigh_ref, slice(WIN_MAX + rows, 2 * WIN_MAX + rows)),
    ):
        out_ref[0] = turn(dext[0, part], cos_ref[part], -sin_ref[part]).astype(BF16)
        out_ref[1] = dext[1, part].astype(BF16)


def attend_back(bounds, queries, grads, attended, lse, low, own, high, ids_query, ids_key, cosine, sine):
    rows = queries.shape[0]
    wide = rows + 2 * WIN_MAX
    column = pl.BlockSpec((rows, LANES), lambda j, b: (0, j))
    fixed = lambda shape: pl.BlockSpec(shape, lambda j, b: (0,) * len(shape))
    return pl.pallas_call(
        attend_back_kernel,
        grid_spec=pltpu.PrefetchScalarGridSpec(
            num_scalar_prefetch=1,
            grid=(D // LANES,),
            in_specs=[
                column,
                column,
                column,
                pl.BlockSpec((PAIRS, 8, rows), lambda j, b: (j, 0, 0)),
                pair_spec(WIN_MAX),
                pair_spec(rows),
                pair_spec(WIN_MAX),
                fixed((8, rows)),
                fixed((wide, 128)),
                fixed((wide, 128)),
                fixed((wide, 128)),
            ],
            out_specs=(column, pair_spec(WIN_MAX), pair_spec(rows), pair_spec(WIN_MAX)),
            scratch_shapes=[pltpu.VMEM((2, wide, LANES), BF16), pltpu.VMEM((2, wide, LANES), F32)],
        ),
        out_shape=(
            jax.ShapeDtypeStruct((rows, D), BF16),
            jax.ShapeDtypeStruct((2, WIN_MAX, D), BF16),
            jax.ShapeDtypeStruct((2, rows, D), BF16),
            jax.ShapeDtypeStruct((2, WIN_MAX, D), BF16),
        ),
        compiler_params=vmem(),
        cost_estimate=cost(12e9, 16e6),
        name="attend_back",
    )(bounds, queries, grads, attended, lse, low, own, high, ids_query, ids_key, cosine, sine)


def feed_kernel(
    o_ref, x_ref, wo_ref, we_ref, ws_ref, bo_ref, be_ref, bs_ref, mod_ref,
    mid_ref, h_ref, z_ref, slope_ref, out_ref,
):
    step = pl.program_id(0)

    @pl.when(step == 0)
    def _():
        middle = x_ref[...].astype(F32) + (product(o_ref[...], wo_ref[...]) + bo_ref[0])
        mid_ref[...] = middle
        normed, _ = normalize(middle)
        h_ref[...] = (normed * (1.0 + mod_ref[0, 3:4]) + mod_ref[0, 2:3]).astype(BF16)
        out_ref[...] = middle + bs_ref[0]

    u = product(h_ref[...], we_ref[...]) + be_ref[0]
    share = 0.5 + 0.5 * lax.erf(u * (0.5**0.5))
    active = (u * share).astype(BF16)
    z_ref[...] = active
    slope_ref[...] = (share + u * (jnp.exp(-0.5 * u * u) * (2.0 * math.pi) ** -0.5)).astype(BF16)
    out_ref[...] += product(active, ws_ref[...])


def feed(layer, attended, stream, square, shrink, bias, modulation):
    rows = stream.shape[0]
    whole = lambda shape: pl.BlockSpec(shape, lambda c: (0,) * len(shape))
    width = STEP_COLUMNS
    return pl.pallas_call(
        feed_kernel,
        grid=(FF // width,),
        in_specs=[
            whole((rows, D)),
            whole((rows, D)),
            pl.BlockSpec((D, D), lambda c: (0, 3)),
            pl.BlockSpec((D, width), lambda c: (0, 4 * D // width + c)),
            pl.BlockSpec((width, D), lambda c: (c, 0)),
            pl.BlockSpec((1, 1, D), lambda c: (layer, 0, 3)),
            pl.BlockSpec((1, 1, width), lambda c: (layer, 0, 4 * D // width + c)),
            pl.BlockSpec((1, 1, D), lambda c: (layer, 0, 8)),
            pl.BlockSpec((1, 4, D), lambda c: (layer, 0, 0)),
        ],
        out_specs=(
            whole((rows, D)),
            whole((rows, D)),
            pl.BlockSpec((rows, width), lambda c: (0, c)),
            pl.BlockSpec((rows, width), lambda c: (0, c)),
            whole((rows, D)),
        ),
        out_shape=(
            jax.ShapeDtypeStruct((rows, D), F32),
            jax.ShapeDtypeStruct((rows, D), BF16),
            jax.ShapeDtypeStruct((rows, FF), BF16),
            jax.ShapeDtypeStruct((rows, FF), BF16),
            jax.ShapeDtypeStruct((rows, D), F32),
        ),
        compiler_params=vmem(),
        cost_estimate=cost(2 * rows * D * (D + 2 * FF), 24e6),
        name="feed",
    )(attended, stream, square, square, shrink, bias, bias, bias, modulation)


def feed_back_kernel(
    g_ref, z_ref, slope_ref, h_ref, mid_ref, o_ref, we_ref, ws_ref, wo_ref, mod_ref,
    dexp_ref, dout_ref, dshr_ref, mid_grad_ref, do_ref, dbe_ref, sums_ref,
    low, turned, total,
):
    step = pl.program_id(0)
    chunks = FF // STEP_COLUMNS

    @pl.when(step == 0)
    def _():
        low[...] = g_ref[...].astype(BF16)
        turned[...] = h_ref[...].T
        total[...] = jnp.zeros_like(total)
        sums_ref[3:4] = jnp.sum(low[...].astype(F32), axis=0, keepdims=True)

    @pl.when(step < chunks)
    def _():
        grad_active = product(low[...], ws_ref[...], MATMUL_RIGHT)
        grad_hidden = (grad_active * slope_ref[...].astype(F32)).astype(BF16)
        dbe_ref[...] = jnp.sum(grad_hidden.astype(F32), axis=0, keepdims=True)
        dshr_ref[...] = product(z_ref[...], low[...], MATMUL_LEFT).astype(BF16)
        dexp_ref[...] = product(turned[...], grad_hidden).astype(BF16)
        total[...] += product(grad_hidden, we_ref[...], MATMUL_RIGHT)

    @pl.when(step == chunks)
    def _():
        normed, inverse = normalize(mid_ref[...])
        grad = total[...]
        sums_ref[0:1] = jnp.sum(grad, axis=0, keepdims=True)
        sums_ref[1:2] = jnp.sum(grad * normed, axis=0, keepdims=True)
        middle = g_ref[...].astype(F32) + normalize_back(grad * (1.0 + mod_ref[0, 3:4]), normed, inverse)
        mid_grad_ref[...] = middle
        low[...] = middle.astype(BF16)
        sums_ref[2:3] = jnp.sum(low[...].astype(F32), axis=0, keepdims=True)
        do_ref[...] = product(low[...], wo_ref[...], MATMUL_RIGHT).astype(BF16)
        turned[...] = o_ref[...].T
        dout_ref[...] = product(turned[...], low[:, :STEP_COLUMNS]).astype(BF16)

    @pl.when(step == chunks + 1)
    def _():
        dout_ref[...] = product(turned[...], low[:, STEP_COLUMNS:]).astype(BF16)


def feed_back(layer, grad, active, slope, hidden_in, middle, attended, square, shrink, modulation):
    rows = grad.shape[0]
    whole = lambda shape: pl.BlockSpec(shape, lambda c: (0,) * len(shape))
    width = STEP_COLUMNS
    chunks = FF // width
    upto = lambda c: jnp.minimum(c, chunks - 1)
    return pl.pallas_call(
        feed_back_kernel,
        grid=(chunks + 2,),
        in_specs=[
            whole((rows, D)),
            pl.BlockSpec((rows, width), lambda c: (0, upto(c))),
            pl.BlockSpec((rows, width), lambda c: (0, upto(c))),
            whole((rows, D)),
            whole((rows, D)),
            whole((rows, D)),
            pl.BlockSpec((D, width), lambda c: (0, 4 * D // width + upto(c))),
            pl.BlockSpec((width, D), lambda c: (upto(c), 0)),
            pl.BlockSpec((D, D), lambda c: (0, 3)),
            pl.BlockSpec((1, 4, D), lambda c: (layer, 0, 0)),
        ],
        out_specs=(
            pl.BlockSpec((D, width), lambda c: (0, upto(c))),
            pl.BlockSpec((D, width), lambda c: (0, jnp.clip(c - chunks, 0, 1))),
            pl.BlockSpec((width, D), lambda c: (upto(c), 0)),
            whole((rows, D)),
            whole((rows, D)),
            pl.BlockSpec((1, width), lambda c: (0, upto(c))),
            whole((4, D)),
        ),
        out_shape=(
            jax.ShapeDtypeStruct((D, FF), BF16),
            jax.ShapeDtypeStruct((D, D), BF16),
            jax.ShapeDtypeStruct((FF, D), BF16),
            jax.ShapeDtypeStruct((rows, D), F32),
            jax.ShapeDtypeStruct((rows, D), BF16),
            jax.ShapeDtypeStruct((1, FF), F32),
            jax.ShapeDtypeStruct((4, D), F32),
        ),
        scratch_shapes=[
            pltpu.VMEM((rows, D), BF16),
            pltpu.VMEM((D, rows), BF16),
            pltpu.VMEM((rows, D), F32),
        ],
        compiler_params=vmem(),
        cost_estimate=cost(4 * rows * D * (D + 2 * FF), 40e6),
        name="feed_back",
    )(grad, active, slope, hidden_in, middle, attended, square, shrink, square, modulation)


def project_back_kernel(
    dq_ref, low_ref, own_ref, high_ref, h_ref, halo_ref, x_ref, mid_grad_ref, w_ref, mod_ref,
    square_ref, out_ref, db_ref, sums_ref,
    turned, total, around, sending, landing, send_sem, recv_sem,
):
    step = pl.program_id(0)
    rows = x_ref.shape[0]
    middle = slice(WIN_MAX, WIN_MAX + rows)
    sources = (sending.at[0], sending.at[1])

    @pl.when(step == 0)
    def _():
        around[...] = jnp.zeros_like(around)
        total[...] = jnp.zeros_like(total)
        greet_beside()

    @pl.when(step < 4)
    def _():
        around[0] += product(low_ref[0], w_ref[...], MATMUL_RIGHT)
        around[1] += product(high_ref[0], w_ref[...], MATMUL_RIGHT)

    @pl.when(step == 3)
    def _():
        sending[...] = around[...].astype(BF16)
        halo_start(sources, landing, send_sem, recv_sem)
        turned[:, :WIN_MAX] = halo_ref[0].T
        turned[:, middle] = h_ref[...].T
        turned[:, WIN_MAX + rows :] = halo_ref[1].T

    @pl.when((step >= 4) & (step < 6))
    def _():
        grad = dq_ref[...]
        db_ref[...] = jnp.sum(grad.astype(F32), axis=0, keepdims=True)
        square_ref[...] = product(turned[:, middle], grad).astype(BF16)
        total[...] += product(grad, w_ref[...], MATMUL_RIGHT)

    @pl.when(step >= 6)
    def _():
        grad = jnp.concatenate([low_ref[0], own_ref[0], high_ref[0]], axis=0)
        db_ref[...] = jnp.sum(grad.astype(F32), axis=0, keepdims=True)
        square_ref[...] = product(turned[...], grad).astype(BF16)
        total[...] += product(own_ref[0], w_ref[...], MATMUL_RIGHT)

    @pl.when(step == 9)
    def _():
        halo_wait(sources, landing, send_sem, recv_sem)
        normed, inverse = normalize(x_ref[...].astype(F32))
        grad = total[...] + landing[0].astype(F32) + landing[1].astype(F32)
        sums_ref[0:1] = jnp.sum(grad, axis=0, keepdims=True)
        sums_ref[1:2] = jnp.sum(grad * normed, axis=0, keepdims=True)
        out_ref[...] = mid_grad_ref[...] + normalize_back(
            grad * (1.0 + mod_ref[0, 1:2]), normed, inverse
        )


def project_back(layer, dq, low, own, high, hidden_in, halo, stream, mid_grad, square, modulation, ident):
    rows = dq.shape[0]
    width = STEP_COLUMNS
    whole = lambda shape: pl.BlockSpec(shape, lambda c: (0,) * len(shape))

    def halves(c):
        at = jnp.where(c < 4, c, jnp.clip(c - 6, 0, 3))
        return (at // 2, 0, at % 2)

    later = pl.BlockSpec((1, rows, width), halves)
    own_columns = lambda c: (0, jnp.clip(c - 4, 0, 5))
    return pl.pallas_call(
        project_back_kernel,
        grid=(10,),
        in_specs=[
            pl.BlockSpec((rows, width), lambda c: (0, jnp.clip(c - 4, 0, 1))),
            later,
            later,
            later,
            whole((rows, D)),
            whole((2, rows, D)),
            whole((rows, D)),
            whole((rows, D)),
            pl.BlockSpec((D, width), lambda c: (0, jnp.where(c < 4, c + 2, c - 4))),
            pl.BlockSpec((1, 4, D), lambda c: (layer, 0, 0)),
        ],
        out_specs=(
            pl.BlockSpec((D, width), own_columns),
            whole((rows, D)),
            pl.BlockSpec((1, width), own_columns),
            whole((2, D)),
        ),
        out_shape=(
            jax.ShapeDtypeStruct((D, 3 * D), BF16),
            jax.ShapeDtypeStruct((rows, D), F32),
            jax.ShapeDtypeStruct((1, 3 * D), F32),
            jax.ShapeDtypeStruct((2, D), F32),
        ),
        scratch_shapes=[
            pltpu.VMEM((D, rows + 2 * WIN_MAX), BF16),
            pltpu.VMEM((rows, D), F32),
            pltpu.VMEM((2, rows, D), F32),
            pltpu.VMEM((2, rows, D), BF16),
            pltpu.VMEM((2, rows, D), BF16),
            pltpu.SemaphoreType.DMA((2,)),
            pltpu.SemaphoreType.DMA((2,)),
        ],
        compiler_params=pltpu.CompilerParams(
            vmem_limit_bytes=56 << 20, collective_id=ident, has_side_effects=True
        ),
        cost_estimate=cost(4 * rows * D * 6 * D, 20e6),
        name="project_back",
    )(dq, low, own, high, hidden_in, halo, stream, mid_grad, square, modulation)


def direct():
    return lax.axis_size("dp") == NZ * NY and lax.axis_size("fsdp") == NX * 2


BOTH = ("dp", "fsdp")


def pack_small(bias, table):
    flat = jnp.concatenate([bias.reshape(-1), table.reshape(-1)])
    flat = jnp.pad(flat, (0, OWN_ROWS[4] * SMALL - flat.shape[0]))
    return flat.reshape(1, OWN_ROWS[4], SMALL)


def unpack_small(whole, lead_row):
    count = lax.axis_size("dp") * lax.axis_size("fsdp")
    flat = whole.reshape(count, -1).astype(F32)
    wide = LAYERS * 9 * D // count
    bias = flat[:, :wide].reshape(count, LAYERS, 9, -1).transpose(1, 2, 0, 3).reshape(LAYERS, 1, 9 * D)
    table = flat[:, wide : wide + LAYERS * LEADS * 4 * D // count].reshape(count, LAYERS, LEADS, -1)
    rows = lax.dynamic_index_in_dim(table, lead_row, 2, keepdims=False)
    return bias, rows.transpose(1, 0, 2).reshape(LAYERS, 4, D)


def plain_fetch(masters, layer):
    square = jnp.concatenate([masters[n][layer].astype(BF16) for n in range(3)], axis=1)
    shrink = masters[3][layer].astype(BF16)
    return (
        lax.all_gather(square, BOTH, axis=0, tiled=True),
        lax.all_gather(shrink, BOTH, axis=0, tiled=True),
    )


def plain_small(masters, lead_row):
    bias = lax.all_gather(masters[4].astype(BF16), BOTH, axis=2, tiled=True)
    table = lax.all_gather(masters[5].astype(BF16), BOTH, axis=2, tiled=True)
    modulation = lax.dynamic_index_in_dim(table, lead_row, 1, keepdims=False)
    return bias.astype(F32).reshape(LAYERS, 1, 9 * D), modulation.astype(F32).reshape(LAYERS, 4, D)


def plain_reduce(whole):
    return lax.psum_scatter(whole, BOTH, scatter_dimension=0, tiled=True).astype(F32)


def reduce_small_inputs(bias_grads, rows_grads, lead_hot):
    count = lax.axis_size("dp") * lax.axis_size("fsdp")
    bias = bias_grads.reshape(LAYERS * 9, count, -1).transpose(1, 0, 2).reshape(count, -1)
    rows = rows_grads.reshape(LAYERS, 1, count, -1) * lead_hot[None, :, None, None]
    rows = rows.transpose(2, 0, 1, 3).reshape(count, -1)
    flat = jnp.concatenate([bias, rows], axis=1)
    used = flat.shape[1]
    flat = jnp.pad(flat, ((0, 0), (0, OWN_ROWS[4] * SMALL - used)))
    return flat.reshape(-1, SMALL).astype(BF16)


def split_small(own):
    count = lax.axis_size("dp") * lax.axis_size("fsdp")
    flat = own.reshape(-1)
    wide = LAYERS * 9 * D // count
    used = wide + LAYERS * LEADS * 4 * D // count
    return flat[:wide].reshape(LAYERS, 9, -1), flat[wide:used].reshape(LAYERS, LEADS, -1)


def bands(segment_ids, segment_starts, padding_mask, offset, rows):
    length = segment_ids.shape[0]
    position = jnp.arange(length, dtype=jnp.int32)
    real = padding_mask == 1
    names = jnp.where(real, segment_ids, length + position)
    fill = jnp.full((WIN_MAX,), -1, jnp.int32)
    wide = lax.dynamic_slice_in_dim(
        jnp.concatenate([fill, names, fill - 1]), offset, rows + 2 * WIN_MAX
    )
    own = lax.dynamic_slice_in_dim(names, offset, rows)
    piece = lambda array: lax.dynamic_slice_in_dim(array, offset, rows).reshape(-1, BAND)
    at = offset + jnp.arange(rows // BAND, dtype=jnp.int32) * BAND
    starts, windows, kept = piece(segment_starts), piece(segment_ids), piece(padding_mask) == 1
    begins = jnp.where(kept[:, 0], starts[:, 0], at)
    ends = jnp.sum((segment_ids[None, :] <= windows[:, -1:]).astype(jnp.int32), axis=1)
    ends = jnp.where(kept[:, -1], ends, at + BAND)
    low = (begins - offset + WIN_MAX) // BAND
    need = (ends - offset + WIN_MAX + BAND - 1) // BAND - low
    return jnp.stack([low, need]), own, wide


def adam_update(weight, gradient, moment, square, step_rate, decay_rate):
    moment = BETA_ONE * moment + (1.0 - BETA_ONE) * gradient
    square = BETA_TWO * square + (1.0 - BETA_TWO) * gradient * gradient
    first_fix = 1.0 - BETA_ONE**STEP
    second_fix = 1.0 - BETA_TWO**STEP
    update = moment / first_fix / (jnp.sqrt(square / second_fix) + ADAM_EPSILON)
    weight = weight - step_rate * (update + decay_rate * weight)
    return (weight, moment, square, weight.astype(jnp.bfloat16))


def shards(
    tokens,
    cotangent,
    segment_ids,
    segment_starts,
    padding_mask,
    lead_index,
    input_weights,
    input_moment,
    input_square,
    output_weights,
    output_moment,
    output_square,
    expand_weights,
    expand_moment,
    expand_square,
    shrink_weights,
    shrink_moment,
    shrink_square,
    bias_vector,
    bias_moment,
    bias_square,
    lead_table,
    lead_moment,
    lead_square,
):
    rows = tokens.shape[0]
    offset = lax.axis_index("fsdp") * rows
    bounds, own_names, wide_names = bands(segment_ids, segment_starts, padding_mask, offset, rows)
    ids_query = jnp.broadcast_to(own_names[:, None], (rows, 128))
    ids_key = jnp.broadcast_to(wide_names[None, :], (8, wide_names.shape[0]))
    ids_query_row = jnp.broadcast_to(own_names[None, :], (8, rows))
    ids_key_column = jnp.broadcast_to(wide_names[:, None], (wide_names.shape[0], 128))
    fill = jnp.zeros((WIN_MAX,), jnp.int32)
    relative = jnp.arange(segment_starts.shape[0], dtype=jnp.int32) - segment_starts
    relative = jnp.concatenate([fill, relative, fill])
    cosine, sine = rotary_tables(
        lax.dynamic_slice_in_dim(relative, offset, rows + 2 * WIN_MAX)
    )
    lead_row = lead_index[0]
    lead_hot = (jnp.arange(LEADS, dtype=jnp.int32) == lead_row).astype(F32)
    masters = (input_weights, output_weights, expand_weights, shrink_weights, bias_vector, lead_table)
    linked = direct()
    if linked:
        small = pack_small(bias_vector, lead_table)
        small_full, *first = alone(
            GatherJob(GATHERED, 0), (small, *masters[:4]), "gather_first", 0
        )
        bias, modulation = unpack_small(small_full, lead_row)
        layers = [first]
    else:
        layers = [plain_fetch(masters, 0)]
        bias, modulation = plain_small(masters, lead_row)
    layers += [plain_fetch(masters, layer) for layer in range(1, LAYERS)]
    stream = tokens
    saved = []
    for layer in range(LAYERS):
        square, shrink = layers[layer]
        queries, own, low, high, first_in, halo = project(
            layer, stream, square, bias, modulation, cosine, sine, 10 + layer
        )
        attended, lse = attend(bounds, queries, low, own, high, ids_query, ids_key)
        middle, second_in, active, slope, result = feed(
            layer, attended, stream, square, shrink, bias, modulation
        )
        saved.append(
            (stream, queries, low, own, high, first_in, halo, attended, lse, middle, second_in, active, slope)
        )
        stream = result
    grad = cotangent
    partials = [None] * LAYERS
    bias_grads = [None] * LAYERS
    rows_grads = [None] * LAYERS
    reduced = [[None] * 4 for _ in range(LAYERS)]
    for layer in reversed(range(LAYERS)):
        square, shrink = layers[layer]
        (
            before, queries, low, own, high, first_in, halo, attended, lse, middle, second_in, active, slope,
        ) = saved[layer]
        expand_grad, output_grad, shrink_grad, mid_grad, attended_grad, expand_bias, sums = feed_back(
            layer, grad, active, slope, second_in, middle, attended, square, shrink, modulation
        )
        dq, low_grad, own_grad, high_grad = attend_back(
            bounds, queries, attended_grad, attended, lse, low, own, high, ids_query_row,
            ids_key_column, cosine, sine,
        )
        input_grad, grad, input_bias, more_sums = project_back(
            layer, dq, low_grad, own_grad, high_grad, first_in, halo, before, mid_grad, square, modulation,
            20 + layer,
        )
        bias_grads[layer] = jnp.concatenate([input_bias[0], sums[2], expand_bias[0], sums[3]])
        rows_grads[layer] = jnp.concatenate([more_sums[0], more_sums[1], sums[0], sums[1]])
        partials[layer] = (input_grad, output_grad, expand_grad, shrink_grad)
        if not linked:
            reduced[layer] = [plain_reduce(whole) for whole in partials[layer]]
        elif layer > 0:
            later_shrink = lax.psum_scatter(shrink_grad, BOTH, scatter_dimension=0, tiled=True)
    if linked:
        small = reduce_small_inputs(jnp.stack(bias_grads), jnp.stack(rows_grads), lead_hot)
        small, later_shrink = lax.optimization_barrier((small, later_shrink))
        reduced[1][3] = later_shrink.astype(F32)
        job = ScatterJob(SCATTERED)
        input_grad, output_grad, expand_grad, shrink_grad = partials[0]
        wide, reduced[0][3] = alone(
            job,
            (*partials[1][:3], expand_grad, shrink_grad, input_grad, output_grad, small),
            "scatter_last",
            1,
        )
        part = lambda n: wide[:, job.first[n] : job.first[n] + WIDTHS[n]]
        reduced[0][:3] = [part(0), part(1), part(2)]
        reduced[1][:3] = [part(5), part(6), part(7)]
        bias_grad, lead_grad = lax.optimization_barrier(split_small(part(4)))
    else:
        bias_grad = lax.psum_scatter(
            jnp.stack(bias_grads).reshape(LAYERS, 9, D), BOTH, scatter_dimension=2, tiled=True
        )
        lead_grad = lax.psum_scatter(
            jnp.stack(rows_grads)[:, None, :] * lead_hot[None, :, None], BOTH, scatter_dimension=2,
            tiled=True,
        )
    moments = (input_moment, output_moment, expand_moment, shrink_moment, bias_moment, lead_moment)
    squares = (input_square, output_square, expand_square, shrink_square, bias_square, lead_square)
    results = []
    for number in range(6):
        if number < 4:
            gradient = jnp.stack([reduced[layer][number] for layer in range(LAYERS)])
        else:
            gradient = (bias_grad, lead_grad)[number - 4]
        results.append(
            adam_update(
                masters[number],
                gradient,
                moments[number],
                squares[number],
                RATE_MATRIX if number < 4 else RATE_VECTOR,
                DECAY if number < 4 else 0.0,
            )
        )
    return (stream, grad, *(array for four in results for array in four))


def solution(mesh):
    rows = P(("dp", "fsdp"), None)
    matrix = P(None, ("dp", "fsdp"), None)
    vector = P(None, None, ("dp", "fsdp"))
    return jax.shard_map(
        shards,
        mesh=mesh,
        in_specs=(rows,) * 2 + (P("dp"),) * 4 + (matrix,) * 12 + (vector,) * 6,
        out_specs=(rows,) * 2 + (matrix,) * 16 + (vector,) * 8,
        check_vma=False,
    )
```

profile of v0, /device:TPU:0, one launch (start us, length us, event | category | flops | bytes accessed | tf_op | source)
XLA Modules:
  0.0 512.4 jit_solution(10287947134137826279)
XLA Ops:
  10.9 1.6 slice.177
  13.5 95.5 %gather_first.1 = (bf16[768,256]{1,0:T(8,128)(2,1)}, bf16[768,6144]{1,0:T(8,128)(2,1)}, bf16[3072,768]{1,0:T(8,128)(2,1)}) custom-call(f32[1,24,256]{2,1,0:T(8,128)} %reshape.312.refs_0_, f32[2,24,2304]{2,1,0:T(8,128)} %refs_1_.1, f32[2,24,768]{2,1,0:T(8,128)} %refs_2_.1, f32[2,24,3072]{2,1,0:T(8,128)} %refs_3_.1, f32[2,96,768]{2,1,0:T(8,128)} %refs_4_.1), custom_call_target="tpu_custom_call" | custom-call | bytes 200000000 | tf_op jit(solution)/shard_map/gather_first/pallas_call | solution.py:623
  109.0 1.2 reshape.322
  115.3 4.9 fusion
  120.2 19.0 %project.2 = (bf16[512,768]{1,0:T(8,128)(2,1)}, bf16[2,512,768]{2,1,0:T(8,128)(2,1)}, bf16[2,512,768]{2,1,0:T(8,128)(2,1)}, bf16[2,512,768]{2,1,0:T(8,128)(2,1)}...) custom-call(bf16[512,768]{1,0:T(8,128)(2,1)} %x_ref.5, bf16[768,6144]{1,0:T(8,128)(2,1)} %get-tuple-element.91.w_ref.wo_ref.we_ref, ...), custom_call_target="tpu_custom_call" | custom-call | flops 4227858432 | bytes 8000000 | tf_op jit(solution)/shard_map/project/pallas_call | solution.py:832
  140.6 12.3 %attend.2 = (bf16[512,768]{1,0:T(8,128)(2,1)}, f32[6,8,512]{2,1,0:T(8,128)}) custom-call(s32[2,4]{1,0:T(2,128)} %pad_add_fusion.bounds_ref, bf16[512,768]{1,0:T(8,128)(2,1)} %get-tuple-element.93.q_ref, bf16[2,512,768]{2,1,0:T(8,128)(2,1)} %get-tuple-element.94.low_ref, bf16[2,512,768]{2,1,0:T(8,128)(2,1)} %get-tuple-element.95.own_ref, ...), custom_call_target="tpu_custom_call" | custom-call | flops 5000000000 | bytes 8000000 | tf_op jit(solution)/shard_map/attend/pallas_call | solution.py:945
  152.9 15.0 %feed.2 = (f32[512,768]{1,0:T(8,128)}, bf16[512,768]{1,0:T(8,128)(2,1)}, bf16[512,3072]{1,0:T(8,128)(2,1)}, bf16[512,3072]{1,0:T(8,128)(2,1)}, f32[512,768]{1,0:T(8,128)}) custom-call(bf16[512,768]{1,0:T(8,128)(2,1)} %get-tuple-element.97.o_ref, bf16[512,768]{1,0:T(8,128)(2,1)} %x_ref.5, bf16[768,6144]{1,0:T(8,128)(2,1)} %get-tuple-element.91.w_ref.wo_ref.we_ref, ...), custom_call_target="tpu_custom_call" | custom-call | flops 5435817984 | bytes 24000000 | tf_op jit(solution)/shard_map/feed/pallas_call | solution.py:1089
  167.9 26.0 %project.3 = (bf16[512,768]{1,0:T(8,128)(2,1)}, bf16[2,512,768]{2,1,0:T(8,128)(2,1)}, bf16[2,512,768]{2,1,0:T(8,128)(2,1)}, bf16[2,512,768]{2,1,0:T(8,128)(2,1)}...) custom-call(f32[512,768]{1,0:T(8,128)} %get-tuple-element.99.x_ref, ...), custom_call_target="tpu_custom_call" | custom-call | flops 4227858432 | bytes 8000000 | tf_op jit(solution)/shard_map/project/pallas_call | solution.py:832
  193.9 12.3 %attend.3 = (bf16[512,768]{1,0:T(8,128)(2,1)}, f32[6,8,512]{2,1,0:T(8,128)}) custom-call(s32[2,4]{1,0:T(2,128)} %pad_add_fusion.bounds_ref, bf16[512,768]{1,0:T(8,128)(2,1)} %get-tuple-element.100.q_ref, bf16[2,512,768]{2,1,0:T(8,128)(2,1)} %get-tuple-element.101.low_ref, bf16[2,512,768]{2,1,0:T(8,128)(2,1)} %get-tuple-element.102.own_ref, ...), custom_call_target="tpu_custom_call" | custom-call | flops 5000000000 | bytes 8000000 | tf_op jit(solution)/shard_map/attend/pallas_call | solution.py:945
  206.2 14.9 %feed.3 = (f32[512,768]{1,0:T(8,128)}, bf16[512,768]{1,0:T(8,128)(2,1)}, bf16[512,3072]{1,0:T(8,128)(2,1)}, bf16[512,3072]{1,0:T(8,128)(2,1)}, f32[512,768]{1,0:T(8,128)}) custom-call(bf16[512,768]{1,0:T(8,128)(2,1)} %get-tuple-element.104.o_ref, f32[512,768]{1,0:T(8,128)} %get-tuple-element.99.x_ref, ...), custom_call_target="tpu_custom_call" | custom-call | flops 5435817984 | bytes 24000000 | tf_op jit(solution)/shard_map/feed/pallas_call | solution.py:1089
  221.1 23.5 %feed_back.2 = (bf16[768,3072]{1,0:T(8,128)(2,1)}, bf16[768,768]{1,0:T(8,128)(2,1)}, bf16[3072,768]{1,0:T(8,128)(2,1)}, f32[512,768]{1,0:T(8,128)}, bf16[512,768...) custom-call(bf16[512,768]{1,0:T(8,128)(2,1)} %g_ref.1, bf16[512,3072]{1,0:T(8,128)(2,1)} %get-tuple-element.106.z_ref, ...), custom_call_target="tpu_custom_call" | custom-call | flops 10871635968 | bytes 40000000 | tf_op jit(solution)/shard_map/feed_back/pallas_call | solution.py:1172
  245.2 1.2 broadcast_in_dim.50.idk_ref
  246.4 23.6 %attend_back.2 = (bf16[512,768]{1,0:T(8,128)(2,1)}, bf16[2,512,768]{2,1,0:T(8,128)(2,1)}, bf16[2,512,768]{2,1,0:T(8,128)(2,1)}, bf16[2,512,768]{2,1,0:T(8,128)(2,1)}) custom-call(s32[2,4]{1,0:T(2,128)} %pad_add_fusion.bounds_ref, bf16[512,768]{1,0:T(8,128)(2,1)} %get-tuple-element.100.q_ref, bf16[512,768]{1,0:T(8,128)(2,1)} %get-tuple-element.110.g_ref, ...), custom_call_target="tpu_custom_call" | custom-call | flops 12000000000 | bytes 16000000 | tf_op jit(solution)/shard_map/attend_back/pallas_call | solution.py:1030
  270.0 32.2 %project_back.2 = (bf16[768,2304]{1,0:T(8,128)(2,1)}, f32[512,768]{1,0:T(8,128)}, f32[1,2304]{1,0:T(1,128)}, f32[2,768]{1,0:T(2,128)}) custom-call(bf16[512,768]{1,0:T(8,128)(2,1)} %get-tuple-element.112.dq_ref, bf16[2,512,768]{2,1,0:T(8,128)(2,1)} %get-tuple-element.113.low_ref, bf16[2,512,768]{2,1,0:T(8,128)(2,1)} %get-tuple-element.114.own_ref, ...), custom_call_target="tpu_custom_call" | custom-call | flops 7247757312 | bytes 20000000 | tf_op jit(solution)/shard_map/project_back/pallas_call | solution.py:1282
  302.1 23.7 %feed_back.3 = (bf16[768,3072]{1,0:T(8,128)(2,1)}, bf16[768,768]{1,0:T(8,128)(2,1)}, bf16[3072,768]{1,0:T(8,128)(2,1)}, f32[512,768]{1,0:T(8,128)}, bf16[512,768...) custom-call(f32[512,768]{1,0:T(8,128)} %get-tuple-element.119.g_ref, ...), custom_call_target="tpu_custom_call" | custom-call | flops 10871635968 | bytes 40000000 | tf_op jit(solution)/shard_map/feed_back/pallas_call | solution.py:1172
  325.9 23.7 %attend_back.3 = (bf16[512,768]{1,0:T(8,128)(2,1)}, bf16[2,512,768]{2,1,0:T(8,128)(2,1)}, bf16[2,512,768]{2,1,0:T(8,128)(2,1)}, bf16[2,512,768]{2,1,0:T(8,128)(2,1)}) custom-call(s32[2,4]{1,0:T(2,128)} %pad_add_fusion.bounds_ref, bf16[512,768]{1,0:T(8,128)(2,1)} %get-tuple-element.93.q_ref, bf16[512,768]{1,0:T(8,128)(2,1)} %get-tuple-element.124.g_ref, ...), custom_call_target="tpu_custom_call" | custom-call | flops 12000000000 | bytes 16000000 | tf_op jit(solution)/shard_map/attend_back/pallas_call | solution.py:1030
  349.6 30.1 %project_back.3 = (bf16[768,2304]{1,0:T(8,128)(2,1)}, f32[512,768]{1,0:T(8,128)}, f32[1,2304]{1,0:T(1,128)}, f32[2,768]{1,0:T(2,128)}) custom-call(bf16[512,768]{1,0:T(8,128)(2,1)} %get-tuple-element.126.dq_ref, bf16[2,512,768]{2,1,0:T(8,128)(2,1)} %get-tuple-element.127.low_ref, bf16[2,512,768]{2,1,0:T(8,128)(2,1)} %get-tuple-element.128.own_ref, ...), custom_call_target="tpu_custom_call" | custom-call | flops 7247757312 | bytes 20000000 | tf_op jit(solution)/shard_map/project_back/pallas_call | solution.py:1282
  383.4 105.0 %scatter_last.1 = (f32[24,12544]{1,0:T(8,128)}, f32[96,768]{1,0:T(8,128)}) custom-call(bf16[768,2304]{1,0:T(8,128)(2,1)} %get-tuple-element.134.refs_0_, bf16[768,768]{1,0:T(8,128)(2,1)} %get-tuple-element.135.refs_1_, bf16[768,3072]{1,0:T(8,128)(2,1)} %get-tuple-element.136.refs_2_, bf16[768,3072]{1,0:T(8,128)(2,1)} %get-tuple-element.137.refs_3_, ...), custom_call_target="tpu_custom_call" | custom-call | bytes 200000000 | tf_op jit(solution)/shard_map/scatter_last/pallas_call | solution.py:623
  488.5 1.2 slice_bitcast_fusion.3
  490.6 1.1 slice_bitcast_fusion.1
  497.7 1.4 fusion.37
  500.0 1.6 fusion.33
  502.2 1.6 fusion.31
  504.2 1.1 copy.169
  (162 shorter events, 23.2 us)
Async XLA Ops:
  7.2 5.4 %copy-start.15 = (f32[2,20,96]{2,0,1:T(2,128)S(1)}, f32[2,20,96]{2,0,1:T(2,128)}, u32[]{:S(2)}) copy-start(f32[2,20,96]{2,0,1:T(2,128)} %param.45) | copy-start | bytes 46084
  7.2 5.5 %copy-start.17 = (f32[2,9,24]{2,0,1:T(2,128)S(1)}, f32[2,9,24]{2,0,1:T(2,128)}, u32[]{:S(2)}) copy-start(f32[2,9,24]{2,0,1:T(2,128)} %param.42) | copy-start | bytes 5188
  7.2 160.7 %all-gather.4.cloned.1.call-start = ((), (), s32[]{:S(2)}) async-start(), calls=%async_computation.1 | async-start | bytes 9732096 | tf_op jit(solution)/shard_map/all_gather | solution.py:1353
  10.9 195.3 %all-gather.6.cloned.1.call-start = ((), (), s32[]{:S(2)}) async-start(), calls=%async_computation.3 | async-start | bytes 4866048 | tf_op jit(solution)/shard_map/all_gather | solution.py:1354
  12.6 370.8 %reduce-scatter.2.cloned.1.call-start = ((), (), s32[]{:S(2)}) async-start(), calls=%async_computation.2 | async-start | bytes 4866048 | tf_op jit(solution)/shard_map/reduce_scatter | solution.py:1515
  110.4 3.2 copy-start.16
  110.4 3.2 copy-start.22
  110.4 3.4 copy-start.23
  349.6 30.2 %copy-start.18 = (f32[4,768]{1,0:T(4,128)S(1)}, f32[4,768]{1,0:T(4,128)}, u32[]{:S(2)}) copy-start(f32[4,768]{1,0:T(4,128)} %get-tuple-element.145) | copy-start | bytes 36868
  349.6 30.2 %copy-start.30 = (f32[2,768]{1,0:T(2,128)S(1)}, f32[2,768]{1,0:T(2,128)}, u32[]{:S(2)}) copy-start(f32[2,768]{1,0:T(2,128)} %get-tuple-element.148) | copy-start | bytes 18436
  349.6 30.4 %copy-start.19 = (f32[4,768]{1,0:T(4,128)S(1)}, f32[4,768]{1,0:T(4,128)}, u32[]{:S(2)}) copy-start(f32[4,768]{1,0:T(4,128)} %get-tuple-element.142) | copy-start | bytes 36868
  488.4 4.2 copy-start.14
  488.4 4.3 copy-start.26
  488.4 4.3 copy-start.27
  488.4 6.8 %copy-start.20 = (f32[2,20,96]{2,0,1:T(2,128)S(1)}, f32[2,20,96]{2,0,1:T(2,128)}, u32[]{:S(2)}) copy-start(f32[2,20,96]{2,0,1:T(2,128)} %param.46) | copy-start | bytes 46084
  488.4 6.8 %copy-start.21 = (f32[2,20,96]{2,0,1:T(2,128)S(1)}, f32[2,20,96]{2,0,1:T(2,128)}, u32[]{:S(2)}) copy-start(f32[2,20,96]{2,0,1:T(2,128)} %param.47) | copy-start | bytes 46084
  488.4 9.2 %copy-start.2 = (f32[2,24,2304]{2,1,0:T(8,128)S(1)}, f32[2,24,2304]{2,1,0:T(8,128)}, u32[]{:S(2)}) copy-start(f32[2,24,2304]{2,1,0:T(8,128)} %refs_1_.1) | copy-start | bytes 1327108
  488.4 9.2 %copy-start.9 = (f32[2,24,2304]{2,1,0:T(8,128)S(1)}, f32[2,24,2304]{2,1,0:T(8,128)}, u32[]{:S(2)}) copy-start(f32[2,24,2304]{2,1,0:T(8,128)} %param.31) | copy-start | bytes 1327108
  488.4 9.2 %copy-start.10 = (f32[2,24,2304]{2,1,0:T(8,128)S(1)}, f32[2,24,2304]{2,1,0:T(8,128)}, u32[]{:S(2)}) copy-start(f32[2,24,2304]{2,1,0:T(8,128)} %param.32) | copy-start | bytes 1327108
  497.7 2.3 copy-start
  497.7 2.3 copy-start.5
  497.7 2.2 copy-start.6
  500.0 2.0 copy-start.8
  500.0 2.2 copy-start.11
  (10 other events, 16.4 us)
Sparse Core Ops, SparseCore 0:
  11.5 103.2 all-gather.3
  118.3 68.9 all-gather.5
  244.7 109.3 reduce-scatter.1
where the time goes:
time: 518 us; the launch traced here: 512 us
  Pallas kernels  457 us (88%)
  local copies, waits for them, and re-layouts  27.1 us (5%)
  between operations  15.7 us (3%)
  other arithmetic  12.8 us (2%)
    pallas_call x2, Pallas kernels, alone(): pl.pallas_call(kernel, out_shape=job.outputs, in_specs=[anywhere] * job.i...  200 us
    pallas_call x2, Pallas kernels, project_back(): pl.pallas_call(project_back_kernel, grid=(10,), in_specs=[pl.BlockSpec((r...  62.3 us
    pallas_call x2, Pallas kernels, attend_back(): pl.pallas_call(attend_back_kernel, grid_spec=pltpu.PrefetchScalarGridSpec...  47.3 us
    pallas_call x2, Pallas kernels, feed_back(): pl.pallas_call(feed_back_kernel, grid=(chunks + 2,), in_specs=[whole((row...  47.2 us
    pallas_call x2, Pallas kernels, project(): pl.pallas_call(project_kernel, grid=(10,), in_specs=[whole((rows, D)), pl...  45 us
    pallas_call x2, Pallas kernels, feed(): pl.pallas_call(feed_kernel, grid=(FF // width,), in_specs=[whole((rows, D...  29.8 us
    pallas_call x2, Pallas kernels, attend(): pl.pallas_call(attend_kernel, grid_spec=pltpu.PrefetchScalarGridSpec(num_...  24.6 us
  transfers between devices with their start and end apart: 3, of which 0 were waited for; matrix products, arithmetic and copies ran while one was open for 4% of the time, Pallas kernels for 61%

commit v1 on v0

--- a/solution.py
+++ b/solution.py
@@ -1368,9 +1368,9 @@
 
 def reduce_small_inputs(bias_grads, rows_grads, lead_hot):
     count = lax.axis_size("dp") * lax.axis_size("fsdp")
-    bias = bias_grads.reshape(LAYERS * 9, count, -1).transpose(1, 0, 2).reshape(count, -1)
+    bias = bias_grads.reshape(LAYERS, 9, count, -1).transpose(2, 1, 0, 3).reshape(count, -1)
     rows = rows_grads.reshape(LAYERS, 1, count, -1) * lead_hot[None, :, None, None]
-    rows = rows.transpose(2, 0, 1, 3).reshape(count, -1)
+    rows = rows.transpose(2, 1, 0, 3).reshape(count, -1)
     flat = jnp.concatenate([bias, rows], axis=1)
     used = flat.shape[1]
     flat = jnp.pad(flat, ((0, 0), (0, OWN_ROWS[4] * SMALL - used)))
@@ -1382,7 +1382,9 @@
     flat = own.reshape(-1)
     wide = LAYERS * 9 * D // count
     used = wide + LAYERS * LEADS * 4 * D // count
-    return flat[:wide].reshape(LAYERS, 9, -1), flat[wide:used].reshape(LAYERS, LEADS, -1)
+    bias = flat[:wide].reshape(9, LAYERS, -1)
+    rows = flat[wide:used].reshape(LEADS, LAYERS, -1)
+    return bias.transpose(1, 0, 2), rows.transpose(1, 0, 2)
 
 
 def bands(segment_ids, segment_starts, padding_mask, offset, rows):
@@ -1528,7 +1530,7 @@
         part = lambda n: wide[:, job.first[n] : job.first[n] + WIDTHS[n]]
         reduced[0][:3] = [part(0), part(1), part(2)]
         reduced[1][:3] = [part(5), part(6), part(7)]
-        bias_grad, lead_grad = lax.optimization_barrier(split_small(part(4)))
+        bias_grad, lead_grad = split_small(part(4))
     else:
         bias_grad = lax.psum_scatter(
             jnp.stack(bias_grads).reshape(LAYERS, 9, D), BOTH, scatter_dimension=2, tiled=True

time: 518 us -> 510 us (0.985)
  Pallas kernels: 457 us -> 450 us
    pallas_call x2, Pallas kernels: 62.3 us -> 50.9 us  [project_back(): pl.pallas_call(project_back_kernel, grid=(10,), in_specs=[pl.BlockSpec((r...]
  transfers between devices with their start and end apart: 3 -> 3, of which waited for: 0 -> 0; matrix products, arithmetic and copies ran while one was open for 4% -> 4% of each run, Pallas kernels for 61% -> 60%
where the time goes in v1:
time: 510 us; the launch traced here: 503 us
  Pallas kernels  450 us (88%)
  local copies, waits for them, and re-layouts  23 us (5%)
  between operations  15.7 us (3%)
  other arithmetic  14 us (3%)
    pallas_call x2, Pallas kernels, alone(): pl.pallas_call(kernel, out_shape=job.outputs, in_specs=[anywhere] * job.i...  204 us
    pallas_call x2, Pallas kernels, project_back(): pl.pallas_call(project_back_kernel, grid=(10,), in_specs=[pl.BlockSpec((r...  50.9 us
    pallas_call x2, Pallas kernels, attend_back(): pl.pallas_call(attend_back_kernel, grid_spec=pltpu.PrefetchScalarGridSpec...  48.7 us
    pallas_call x2, Pallas kernels, feed_back(): pl.pallas_call(feed_back_kernel, grid=(chunks + 2,), in_specs=[whole((row...  47.2 us
    pallas_call x2, Pallas kernels, project(): pl.pallas_call(project_kernel, grid=(10,), in_specs=[whole((rows, D)), pl...  43.3 us
    pallas_call x2, Pallas kernels, feed(): pl.pallas_call(feed_kernel, grid=(FF // width,), in_specs=[whole((rows, D...  29.8 us
    pallas_call x2, Pallas kernels, attend(): pl.pallas_call(attend_kernel, grid_spec=pltpu.PrefetchScalarGridSpec(num_...  26.2 us
  transfers between devices with their start and end apart: 3, of which 0 were waited for; matrix products, arithmetic and copies ran while one was open for 4% of the time, Pallas kernels for 60%

profile of v1, /device:TPU:0, one launch (start us, length us, event | category | flops | bytes accessed | tf_op | source)
XLA Modules:
  0.0 502.9 jit_solution(4966934346336506389)
XLA Ops:
  10.9 1.6 slice.186
  13.5 95.5 %gather_first.1 = (bf16[768,256]{1,0:T(8,128)(2,1)}, bf16[768,6144]{1,0:T(8,128)(2,1)}, bf16[3072,768]{1,0:T(8,128)(2,1)}) custom-call(f32[1,24,256]{2,1,0:T(8,128)} %reshape.315.refs_0_, f32[2,24,2304]{2,1,0:T(8,128)} %refs_1_.1, f32[2,24,768]{2,1,0:T(8,128)} %refs_2_.1, f32[2,24,3072]{2,1,0:T(8,128)} %refs_3_.1, f32[2,96,768]{2,1,0:T(8,128)} %refs_4_.1), custom_call_target="tpu_custom_call" | custom-call | bytes 200000000 | tf_op jit(solution)/shard_map/gather_first/pallas_call | solution.py:623
  109.0 1.2 reshape.323
  115.3 4.9 fusion
  120.2 19.0 %project.2 = (bf16[512,768]{1,0:T(8,128)(2,1)}, bf16[2,512,768]{2,1,0:T(8,128)(2,1)}, bf16[2,512,768]{2,1,0:T(8,128)(2,1)}, bf16[2,512,768]{2,1,0:T(8,128)(2,1)}...) custom-call(bf16[512,768]{1,0:T(8,128)(2,1)} %x_ref.5, bf16[768,6144]{1,0:T(8,128)(2,1)} %get-tuple-element.89.w_ref.wo_ref.we_ref, ...), custom_call_target="tpu_custom_call" | custom-call | flops 4227858432 | bytes 8000000 | tf_op jit(solution)/shard_map/project/pallas_call | solution.py:832
  140.7 13.1 %attend.2 = (bf16[512,768]{1,0:T(8,128)(2,1)}, f32[6,8,512]{2,1,0:T(8,128)}) custom-call(s32[2,4]{1,0:T(2,128)} %pad_add_fusion.bounds_ref, bf16[512,768]{1,0:T(8,128)(2,1)} %get-tuple-element.91.q_ref, bf16[2,512,768]{2,1,0:T(8,128)(2,1)} %get-tuple-element.92.low_ref, bf16[2,512,768]{2,1,0:T(8,128)(2,1)} %get-tuple-element.93.own_ref, ...), custom_call_target="tpu_custom_call" | custom-call | flops 5000000000 | bytes 8000000 | tf_op jit(solution)/shard_map/attend/pallas_call | solution.py:945
  153.8 14.9 %feed.2 = (f32[512,768]{1,0:T(8,128)}, bf16[512,768]{1,0:T(8,128)(2,1)}, bf16[512,3072]{1,0:T(8,128)(2,1)}, bf16[512,3072]{1,0:T(8,128)(2,1)}, f32[512,768]{1,0:T(8,128)}) custom-call(bf16[512,768]{1,0:T(8,128)(2,1)} %get-tuple-element.95.o_ref, bf16[512,768]{1,0:T(8,128)(2,1)} %x_ref.5, bf16[768,6144]{1,0:T(8,128)(2,1)} %get-tuple-element.89.w_ref.wo_ref.we_ref, ...), custom_call_target="tpu_custom_call" | custom-call | flops 5435817984 | bytes 24000000 | tf_op jit(solution)/shard_map/feed/pallas_call | solution.py:1089
  168.7 24.2 %project.3 = (bf16[512,768]{1,0:T(8,128)(2,1)}, bf16[2,512,768]{2,1,0:T(8,128)(2,1)}, bf16[2,512,768]{2,1,0:T(8,128)(2,1)}, bf16[2,512,768]{2,1,0:T(8,128)(2,1)}...) custom-call(f32[512,768]{1,0:T(8,128)} %get-tuple-element.97.x_ref, ...), custom_call_target="tpu_custom_call" | custom-call | flops 4227858432 | bytes 8000000 | tf_op jit(solution)/shard_map/project/pallas_call | solution.py:832
  192.9 13.1 %attend.3 = (bf16[512,768]{1,0:T(8,128)(2,1)}, f32[6,8,512]{2,1,0:T(8,128)}) custom-call(s32[2,4]{1,0:T(2,128)} %pad_add_fusion.bounds_ref, bf16[512,768]{1,0:T(8,128)(2,1)} %get-tuple-element.98.q_ref, bf16[2,512,768]{2,1,0:T(8,128)(2,1)} %get-tuple-element.99.low_ref, bf16[2,512,768]{2,1,0:T(8,128)(2,1)} %get-tuple-element.100.own_ref, ...), custom_call_target="tpu_custom_call" | custom-call | flops 5000000000 | bytes 8000000 | tf_op jit(solution)/shard_map/attend/pallas_call | solution.py:945
  206.1 14.8 %feed.3 = (f32[512,768]{1,0:T(8,128)}, bf16[512,768]{1,0:T(8,128)(2,1)}, bf16[512,3072]{1,0:T(8,128)(2,1)}, bf16[512,3072]{1,0:T(8,128)(2,1)}, f32[512,768]{1,0:T(8,128)}) custom-call(bf16[512,768]{1,0:T(8,128)(2,1)} %get-tuple-element.102.o_ref, f32[512,768]{1,0:T(8,128)} %get-tuple-element.97.x_ref, ...), custom_call_target="tpu_custom_call" | custom-call | flops 5435817984 | bytes 24000000 | tf_op jit(solution)/shard_map/feed/pallas_call | solution.py:1089
  220.9 23.5 %feed_back.2 = (bf16[768,3072]{1,0:T(8,128)(2,1)}, bf16[768,768]{1,0:T(8,128)(2,1)}, bf16[3072,768]{1,0:T(8,128)(2,1)}, f32[512,768]{1,0:T(8,128)}, bf16[512,768...) custom-call(bf16[512,768]{1,0:T(8,128)(2,1)} %g_ref.1, bf16[512,3072]{1,0:T(8,128)(2,1)} %get-tuple-element.104.z_ref, ...), custom_call_target="tpu_custom_call" | custom-call | flops 10871635968 | bytes 40000000 | tf_op jit(solution)/shard_map/feed_back/pallas_call | solution.py:1172
  245.1 1.2 broadcast_in_dim.50.idk_ref
  246.3 24.3 %attend_back.2 = (bf16[512,768]{1,0:T(8,128)(2,1)}, bf16[2,512,768]{2,1,0:T(8,128)(2,1)}, bf16[2,512,768]{2,1,0:T(8,128)(2,1)}, bf16[2,512,768]{2,1,0:T(8,128)(2,1)}) custom-call(s32[2,4]{1,0:T(2,128)} %pad_add_fusion.bounds_ref, bf16[512,768]{1,0:T(8,128)(2,1)} %get-tuple-element.98.q_ref, bf16[512,768]{1,0:T(8,128)(2,1)} %get-tuple-element.108.g_ref, ...), custom_call_target="tpu_custom_call" | custom-call | flops 12000000000 | bytes 16000000 | tf_op jit(solution)/shard_map/attend_back/pallas_call | solution.py:1030
  270.6 27.5 %project_back.2 = (bf16[768,2304]{1,0:T(8,128)(2,1)}, f32[512,768]{1,0:T(8,128)}, f32[1,2304]{1,0:T(1,128)}, f32[2,768]{1,0:T(2,128)}) custom-call(bf16[512,768]{1,0:T(8,128)(2,1)} %get-tuple-element.110.dq_ref, bf16[2,512,768]{2,1,0:T(8,128)(2,1)} %get-tuple-element.111.low_ref, bf16[2,512,768]{2,1,0:T(8,128)(2,1)} %get-tuple-element.112.own_ref, ...), custom_call_target="tpu_custom_call" | custom-call | flops 7247757312 | bytes 20000000 | tf_op jit(solution)/shard_map/project_back/pallas_call | solution.py:1282
  298.1 23.7 %feed_back.3 = (bf16[768,3072]{1,0:T(8,128)(2,1)}, bf16[768,768]{1,0:T(8,128)(2,1)}, bf16[3072,768]{1,0:T(8,128)(2,1)}, f32[512,768]{1,0:T(8,128)}, bf16[512,768...) custom-call(f32[512,768]{1,0:T(8,128)} %get-tuple-element.117.g_ref, ...), custom_call_target="tpu_custom_call" | custom-call | flops 10871635968 | bytes 40000000 | tf_op jit(solution)/shard_map/feed_back/pallas_call | solution.py:1172
  321.8 24.4 %attend_back.3 = (bf16[512,768]{1,0:T(8,128)(2,1)}, bf16[2,512,768]{2,1,0:T(8,128)(2,1)}, bf16[2,512,768]{2,1,0:T(8,128)(2,1)}, bf16[2,512,768]{2,1,0:T(8,128)(2,1)}) custom-call(s32[2,4]{1,0:T(2,128)} %pad_add_fusion.bounds_ref, bf16[512,768]{1,0:T(8,128)(2,1)} %get-tuple-element.91.q_ref, bf16[512,768]{1,0:T(8,128)(2,1)} %get-tuple-element.122.g_ref, ...), custom_call_target="tpu_custom_call" | custom-call | flops 12000000000 | bytes 16000000 | tf_op jit(solution)/shard_map/attend_back/pallas_call | solution.py:1030
  346.2 23.4 %project_back.3 = (bf16[768,2304]{1,0:T(8,128)(2,1)}, f32[512,768]{1,0:T(8,128)}, f32[1,2304]{1,0:T(1,128)}, f32[2,768]{1,0:T(2,128)}) custom-call(bf16[512,768]{1,0:T(8,128)(2,1)} %get-tuple-element.124.dq_ref, bf16[2,512,768]{2,1,0:T(8,128)(2,1)} %get-tuple-element.125.low_ref, bf16[2,512,768]{2,1,0:T(8,128)(2,1)} %get-tuple-element.126.own_ref, ...), custom_call_target="tpu_custom_call" | custom-call | flops 7247757312 | bytes 20000000 | tf_op jit(solution)/shard_map/project_back/pallas_call | solution.py:1282
  373.7 108.6 %scatter_last.1 = (f32[24,12544]{1,0:T(8,128)}, f32[96,768]{1,0:T(8,128)}) custom-call(bf16[768,2304]{1,0:T(8,128)(2,1)} %get-tuple-element.132.refs_0_, bf16[768,768]{1,0:T(8,128)(2,1)} %get-tuple-element.133.refs_1_, bf16[768,3072]{1,0:T(8,128)(2,1)} %get-tuple-element.134.refs_2_, bf16[768,3072]{1,0:T(8,128)(2,1)} %get-tuple-element.135.refs_3_, ...), custom_call_target="tpu_custom_call" | custom-call | bytes 200000000 | tf_op jit(solution)/shard_map/scatter_last/pallas_call | solution.py:623
  482.4 1.2 slice_bitcast_fusion.3
  484.5 1.1 slice_bitcast_fusion.1
  488.3 1.4 fusion.37
  490.6 1.6 fusion.33
  492.8 1.6 fusion.31
  494.7 1.1 copy.98
  (152 shorter events, 20.3 us)
Async XLA Ops:
  7.2 5.4 %copy-start.15 = (f32[2,20,96]{2,0,1:T(2,128)S(1)}, f32[2,20,96]{2,0,1:T(2,128)}, u32[]{:S(2)}) copy-start(f32[2,20,96]{2,0,1:T(2,128)} %param.45) | copy-start | bytes 46084
  7.2 5.5 %copy-start.17 = (f32[2,9,24]{2,0,1:T(2,128)S(1)}, f32[2,9,24]{2,0,1:T(2,128)}, u32[]{:S(2)}) copy-start(f32[2,9,24]{2,0,1:T(2,128)} %param.42) | copy-start | bytes 5188
  7.2 161.5 %all-gather.4.cloned.1.call-start = ((), (), s32[]{:S(2)}) async-start(), calls=%async_computation.1 | async-start | bytes 9732096 | tf_op jit(solution)/shard_map/all_gather | solution.py:1353
  10.9 195.2 %all-gather.6.cloned.1.call-start = ((), (), s32[]{:S(2)}) async-start(), calls=%async_computation.3 | async-start | bytes 4866048 | tf_op jit(solution)/shard_map/all_gather | solution.py:1354
  12.6 361.2 %reduce-scatter.2.cloned.1.call-start = ((), (), s32[]{:S(2)}) async-start(), calls=%async_computation.2 | async-start | bytes 4866048 | tf_op jit(solution)/shard_map/reduce_scatter | solution.py:1517
  110.4 3.2 copy-start.16
  110.4 3.2 copy-start.22
  110.4 3.4 copy-start.23
  346.2 23.5 %copy-start.18 = (f32[4,768]{1,0:T(4,128)S(1)}, f32[4,768]{1,0:T(4,128)}, u32[]{:S(2)}) copy-start(f32[4,768]{1,0:T(4,128)} %get-tuple-element.143) | copy-start | bytes 36868
  346.2 23.5 %copy-start.30 = (f32[2,768]{1,0:T(2,128)S(1)}, f32[2,768]{1,0:T(2,128)}, u32[]{:S(2)}) copy-start(f32[2,768]{1,0:T(2,128)} %get-tuple-element.146) | copy-start | bytes 18436
  346.2 23.6 %copy-start.19 = (f32[4,768]{1,0:T(4,128)S(1)}, f32[4,768]{1,0:T(4,128)}, u32[]{:S(2)}) copy-start(f32[4,768]{1,0:T(4,128)} %get-tuple-element.140) | copy-start | bytes 36868
  369.6 2.5 copy-start.29
  369.6 2.5 copy-start.25
  482.3 4.1 copy-start.14
  482.3 4.5 copy-start.26
  482.4 4.5 copy-start.27
  482.4 5.1 %copy-start.20 = (f32[2,20,96]{2,0,1:T(2,128)S(1)}, f32[2,20,96]{2,0,1:T(2,128)}, u32[]{:S(2)}) copy-start(f32[2,20,96]{2,0,1:T(2,128)} %param.46) | copy-start | bytes 46084
  482.4 5.1 %copy-start.21 = (f32[2,20,96]{2,0,1:T(2,128)S(1)}, f32[2,20,96]{2,0,1:T(2,128)}, u32[]{:S(2)}) copy-start(f32[2,20,96]{2,0,1:T(2,128)} %param.47) | copy-start | bytes 46084
  482.4 5.8 %copy-start.2 = (f32[2,24,2304]{2,1,0:T(8,128)S(1)}, f32[2,24,2304]{2,1,0:T(8,128)}, u32[]{:S(2)}) copy-start(f32[2,24,2304]{2,1,0:T(8,128)} %refs_1_.1) | copy-start | bytes 1327108
  482.4 5.8 %copy-start.9 = (f32[2,24,2304]{2,1,0:T(8,128)S(1)}, f32[2,24,2304]{2,1,0:T(8,128)}, u32[]{:S(2)}) copy-start(f32[2,24,2304]{2,1,0:T(8,128)} %param.31) | copy-start | bytes 1327108
  482.4 5.8 %copy-start.10 = (f32[2,24,2304]{2,1,0:T(8,128)S(1)}, f32[2,24,2304]{2,1,0:T(8,128)}, u32[]{:S(2)}) copy-start(f32[2,24,2304]{2,1,0:T(8,128)} %param.32) | copy-start | bytes 1327108
  488.3 2.3 copy-start
  488.3 2.3 copy-start.5
  488.3 2.2 copy-start.6
  (10 other events, 18.2 us)
Sparse Core Ops, SparseCore 0:
  11.5 103.3 all-gather.3
  118.3 69.0 all-gather.5
  244.6 110.2 reduce-scatter.1
